TPU v7x, 32 devices: a whole 2x2x4 slice. The times are simulated.
32 devices in a mesh: row: 8 (over y, x, core), col: 4 (over z).
Axes of the slice: x: 2, y: 2, z: 4, core: 2. Of those that a mesh axis runs over, the one named last changes fastest.
Arguments:
- features: bfloat16 [8192, 256], P(('row', 'col')), may hold values from -6 to 6
- adjacency: bfloat16 [32, 96, 128, 128], P(('row', 'col')), may hold values from -0.09375 to 0.09375
- tile_row: int32 [32, 96], P(('row', 'col')), may hold values from 0 to 7, as said below
- tile_column: int32 [32, 96], P(('row', 'col')), may hold values from 0 to 15, as said below
- tile_count: int32 [32], P(('row', 'col')), may hold values from 1 to 96, as said below
- weight_in: bfloat16 [256, 1024], replicated, may hold values from -0.375 to 0.375
- bias_in: float32 [1024], replicated, may hold values from -3 to 3
- weight_out: bfloat16 [1024, 256], replicated, may hold values from -0.25 to 0.25
- bias_out: float32 [256], replicated, may hold values from -3 to 3
Outputs:
- updated: bfloat16 [8192, 256], P(('row', 'col'))
Inputs may be any that keep to these rules, and one draw needn't show every extreme that they name: `tile_row`: for every device and slot s < tile_count, the block row i and block column j of step one satisfy i >= j, and no device names one pair twice. Slots at or beyond tile_count hold coordinates in range that are not part of A. Every device of the highest index along row holds exactly 96 tiles. `tile_column`: see tile_row. `tile_count`: every device of the highest index along row has the most.
All inputs are finite; a program needn't handle non-finite values.
Results may differ from a plain program's by a relative error of at most 0.0056.
Values may be sent and summed in bfloat16 or wider, within the bound.
A program may use at most 128 MiB of HBM per device.

v0:
```python
import math

import jax
import jax.numpy as jnp
from jax import lax
from jax.sharding import PartitionSpec as P

TILE = 128


def gather_rows(features):
    return lax.all_gather(features, "col", axis=0, tiled=True)


def gather_columns(features):
    return lax.all_gather(features, "row", axis=0, tiled=True)


def reduce_rows(partial_value):
    return lax.psum_scatter(partial_value, "col", scatter_dimension=0, tiled=True)


def reduce_columns(partial_value):
    return lax.psum_scatter(partial_value, "row", scatter_dimension=0, tiled=True)


def accumulate(tile_groups, live_groups, jobs):

    def one_group(carry, inputs):
        tile_block = inputs[0]
        live_block = inputs[1]
        direction = jobs[0][0]
        panel_blocks = jobs[0][1]
        out_count = jobs[0][4]
        source_block = inputs[2]
        target_block = inputs[3]
        source_hot = (
            source_block[:, None] == jnp.arange(panel_blocks.shape[0], dtype=jnp.int32)[None, :]
        ).astype(jnp.bfloat16)
        picked = jnp.einsum(
            "gk,kbf->gbf", source_hot, panel_blocks, preferred_element_type=jnp.float32
        ).astype(jnp.bfloat16)
        if direction == "forward":
            contrib = jnp.einsum(
                "gab,gbf->gaf", tile_block, picked, preferred_element_type=jnp.float32
            )
        else:
            contrib = jnp.einsum(
                "gab,gaf->gbf", tile_block, picked, preferred_element_type=jnp.float32
            )
        target_hot = (
            target_block[:, None] == jnp.arange(out_count, dtype=jnp.int32)[None, :]
        ).astype(jnp.float32) * live_block[:, None]
        added = jnp.einsum("gk,gaf->kaf", target_hot, contrib, precision=lax.Precision.HIGHEST)
        results = [carry[0] + added]
        return (tuple(results), None)

    starts = tuple(
        (jnp.zeros((job[4], job[1].shape[1], job[1].shape[2]), jnp.float32) for job in jobs)
    )
    scanned = [tile_groups, live_groups]
    for job in jobs:
        scanned.append(job[2])
        scanned.append(job[3])
    totals, _ = lax.scan(one_group, starts, tuple(scanned))
    return totals


def shards(
    features, adjacency, tile_row, tile_column, tile_count, weight_in, bias_in, weight_out, bias_out
):
    row_size = lax.axis_size("row")
    col_size = lax.axis_size("col")
    block_count = features.shape[0] // TILE
    width = features.shape[1]
    row_blocks = block_count * col_size
    col_blocks = block_count * row_size
    tiles_here = adjacency[0]
    local_rows = tile_row[0]
    local_cols = tile_column[0]
    count = tile_count[0]
    capacity = tiles_here.shape[0]
    group = math.gcd(capacity, 64)
    rounds = capacity // group
    live = (jnp.arange(capacity, dtype=jnp.int32) < count).astype(jnp.float32)
    live_groups = live.reshape(rounds, group)
    tile_groups = tiles_here.reshape(rounds, group, TILE, TILE)
    row_groups = local_rows.reshape(rounds, group)
    col_groups = local_cols.reshape(rounds, group)
    row_panel = gather_rows(features).reshape(row_blocks, TILE, width)
    to_cols = accumulate(
        tile_groups, live_groups, (("backward", row_panel, row_groups, col_groups, col_blocks),)
    )[0]
    column_panel = gather_columns(features).reshape(col_blocks, TILE, width)
    col_sum = reduce_columns(to_cols.reshape(col_blocks * TILE, width))
    to_rows = accumulate(
        tile_groups, live_groups, (("forward", column_panel, col_groups, row_groups, row_blocks),)
    )[0]
    row_sum = reduce_rows(to_rows.reshape(row_blocks * TILE, width))
    combined = (features.astype(jnp.float32) + row_sum + col_sum).astype(jnp.bfloat16)
    hidden = jax.nn.relu(
        jnp.dot(combined, weight_in, preferred_element_type=jnp.float32) + bias_in
    ).astype(jnp.bfloat16)
    updated = jnp.dot(hidden, weight_out, preferred_element_type=jnp.float32) + bias_out
    return updated.astype(jnp.bfloat16)


def solution(mesh):
    placed = (
        P(("row", "col"), None),
        P(("row", "col"), None, None, None),
        P(("row", "col"), None),
        P(("row", "col"), None),
        P(("row", "col")),
        P(),
        P(),
        P(),
        P(),
    )
    return jax.shard_map(
        shards, mesh=mesh, in_specs=placed, out_specs=P(("row", "col"), None), check_vma=False
    )
```

profile of v0, /device:TPU:6, one launch (start us, length us, event | category | flops | bytes accessed | tf_op | source)
XLA Modules:
  0.0 149.9 jit_solution(8173620761844741485)
XLA Ops:
  6.5 0.0 copy-start
  6.5 0.0 all-gather.2.cloned.1.call-start
  6.5 0.7 all-gather.2.cloned.1.call-update
  7.3 0.0 reduce-scatter.5.cloned.1.call-start
  7.3 16.1 %all_gather.7 = bf16[1024,256]{1,0:T(8,128)(2,1)S(1)} all-gather(bf16[256,256]{1,0:T(8,128)(2,1)} %param.13), channel_id=1, replica_groups=mesh['row'=8,'col'=4] {'col'}, dimensions={0}, use_global_device_ids=true | all-gather | bytes 655360 | tf_op jit(solution)/shard_map/all_gather | solution.py:12
  23.4 0.6 broadcast.39
  24.0 1.4 reduce.6
  25.4 0.1 reshape_squeeze.11
  25.5 1.4 reduce.7
  26.8 0.1 reshape_squeeze.9
  27.6 38.3 %while.23 = (s32[]{:T(128)}, f32[16,128,256]{2,0,1:T(8,128)S(1)}, s32[3,32]{1,0:T(4,128)S(1)}, f32[3,32]{1,0:T(4,128)S(1)}, bf16[3,32,128,128]{3,2,1,0:T(8,128)(...) while((s32[]{:T(128)}, f32[16,128,256]{2,0,1:T(8,128)S(1)}, ...), condition=%wide.region_4.5_spmd.clone, body=%wide.region_3.4_spmd.clone.sunk | while | flops 487589120 | bytes 18351856 | solution.py:65
  27.6 0.8 fusion.91
  28.4 4.9 %fusion.92 = f32[32,128,256]{2,1,0:T(8,128)} fusion(bf16[32,128,256]{2,0,1:T(8,128)(2,1)S(1)} %fusion.91, bf16[3,32,128,128]{3,2,1,0:T(8,128)(2,1)} %get-tuple-element.277, s32[]{:T(128)} %get-tuple-element.264), kind=kOutput, calls=%fused_computation.29.clone.1 | convolution fusion | flops 268435456 | bytes 7340544 | tf_op jit(solution)/shard_map/while/body/eval_jaxpr/gab,gaf->gbf/dot_general | solution.py:48
  33.3 7.1 %select_add_fusion.2 = f32[16,128,256]{2,0,1:T(8,128)S(1)} fusion(f32[16,128,256]{2,0,1:T(8,128)S(1)} %get-tuple-element.265, f32[32,128,256]{2,1,0:T(8,128)} %fusion.92, pred[]{:T(512)S(6)} %compare.7, f32[32]{0:T(128)S(1)} %fusion.93, s32[32]{0:T(128)S(1)} %get-tuple-element.254), kind=kOutput, calls=%fused_computation.30.clone.1 | convolution fusion | flops 202376192 | bytes 8388865 | tf_op jit(solution)/shard_map/while/body/eval_jaxpr/gk,gaf->kaf/dot_general | solution.py:54
  40.4 0.8 fusion.91
  41.1 4.9 %fusion.92 = f32[32,128,256]{2,1,0:T(8,128)} fusion(bf16[32,128,256]{2,0,1:T(8,128)(2,1)S(1)} %fusion.91, bf16[3,32,128,128]{3,2,1,0:T(8,128)(2,1)} %get-tuple-element.277, s32[]{:T(128)} %get-tuple-element.264), kind=kOutput, calls=%fused_computation.29.clone.1 | convolution fusion | flops 268435456 | bytes 7340544 | tf_op jit(solution)/shard_map/while/body/eval_jaxpr/gab,gaf->gbf/dot_general | solution.py:48
  46.0 7.1 %select_add_fusion.2 = f32[16,128,256]{2,0,1:T(8,128)S(1)} fusion(f32[16,128,256]{2,0,1:T(8,128)S(1)} %get-tuple-element.265, f32[32,128,256]{2,1,0:T(8,128)} %fusion.92, pred[]{:T(512)S(6)} %compare.7, f32[32]{0:T(128)S(1)} %fusion.93, s32[32]{0:T(128)S(1)} %get-tuple-element.254), kind=kOutput, calls=%fused_computation.30.clone.1 | convolution fusion | flops 202376192 | bytes 8388865 | tf_op jit(solution)/shard_map/while/body/eval_jaxpr/gk,gaf->kaf/dot_general | solution.py:54
  53.1 0.8 fusion.91
  53.9 4.9 %fusion.92 = f32[32,128,256]{2,1,0:T(8,128)} fusion(bf16[32,128,256]{2,0,1:T(8,128)(2,1)S(1)} %fusion.91, bf16[3,32,128,128]{3,2,1,0:T(8,128)(2,1)} %get-tuple-element.277, s32[]{:T(128)} %get-tuple-element.264), kind=kOutput, calls=%fused_computation.29.clone.1 | convolution fusion | flops 268435456 | bytes 7340544 | tf_op jit(solution)/shard_map/while/body/eval_jaxpr/gab,gaf->gbf/dot_general | solution.py:48
  58.8 7.1 %select_add_fusion.2 = f32[16,128,256]{2,0,1:T(8,128)S(1)} fusion(f32[16,128,256]{2,0,1:T(8,128)S(1)} %get-tuple-element.265, f32[32,128,256]{2,1,0:T(8,128)} %fusion.92, pred[]{:T(512)S(6)} %compare.7, f32[32]{0:T(128)S(1)} %fusion.93, s32[32]{0:T(128)S(1)} %get-tuple-element.254), kind=kOutput, calls=%fused_computation.30.clone.1 | convolution fusion | flops 202376192 | bytes 8388865 | tf_op jit(solution)/shard_map/while/body/eval_jaxpr/gk,gaf->kaf/dot_general | solution.py:54
  65.9 2.5 %copy.11 = f32[16,128,256]{2,1,0:T(8,128)} copy(f32[16,128,256]{2,0,1:T(8,128)S(1)} %get-tuple-element.80) | data formatting | bytes 4194304 | tf_op jit(solution)/shard_map/while | solution.py:65
  68.4 0.0 reduce-scatter.5.cloned.1.call-update
  68.4 0.2 reduce-scatter.3.cloned.1.call-start
  68.7 0.0 all-gather.2.cloned.1.call-done
  68.7 41.0 %while.22 = (s32[]{:T(128)}, f32[8,128,256]{2,0,1:T(8,128)S(1)}, s32[3,32]{1,0:T(4,128)S(1)}, f32[3,32]{1,0:T(4,128)S(1)}, bf16[3,32,128,128]{3,2,1,0:T(8,128)(2...) while((s32[]{:T(128)}, f32[8,128,256]{2,0,1:T(8,128)S(1)}, ...), condition=%wide.region_1.2_spmd.clone, body=%wide.region_0.1_spmd.clone.sunk | while | flops 403178496 | bytes 16778992 | solution.py:65
  68.7 2.1 %fusion.81 = bf16[32,128,256]{2,0,1:T(8,128)(2,1)S(1)} fusion(bf16[16,128,256]{2,1,0:T(8,128)(2,1)} %get-tuple-element.306, s32[32]{0:T(128)S(1)} %get-tuple-element.244), kind=kOutput, calls=%fused_computation.6.clone.1 | convolution fusion | flops 33554944 | bytes 3145856 | tf_op jit(solution)/shard_map/while/body/eval_jaxpr/gk,kbf->gbf/dot_general | solution.py:40
  70.8 4.7 %fusion.82 = f32[32,128,256]{2,1,0:T(8,128)} fusion(bf16[32,128,256]{2,0,1:T(8,128)(2,1)S(1)} %fusion.81, bf16[3,32,128,128]{3,2,1,0:T(8,128)(2,1)} %get-tuple-element.304, s32[]{:T(128)} %get-tuple-element.291), kind=kOutput, calls=%fused_computation.3.clone.1 | convolution fusion | flops 268435456 | bytes 7340544 | tf_op jit(solution)/shard_map/while/body/eval_jaxpr/gab,gbf->gaf/dot_general | solution.py:44
  75.5 6.8 %fusion.84 = f32[8,128,256]{2,0,1:T(8,128)S(1)} fusion(f32[32,128,256]{2,1,0:T(8,128)} %fusion.82, f32[8,128,256]{2,0,1:T(8,128)S(1)} %get-tuple-element.292, pred[]{:T(512)S(6)} %compare.6, f32[32]{0:T(128)S(1)} %fusion.83, s32[32]{0:T(128)S(1)} %get-tuple-element.245), kind=kOutput, calls=%fused_computation.4.clone.1 | convolution fusion | flops 101188096 | bytes 6291713 | tf_op jit(solution)/shard_map/while/body/eval_jaxpr/gk,gaf->kaf/dot_general | solution.py:54
  82.4 2.1 %fusion.81 = bf16[32,128,256]{2,0,1:T(8,128)(2,1)S(1)} fusion(bf16[16,128,256]{2,1,0:T(8,128)(2,1)} %get-tuple-element.306, s32[32]{0:T(128)S(1)} %get-tuple-element.244), kind=kOutput, calls=%fused_computation.6.clone.1 | convolution fusion | flops 33554944 | bytes 3145856 | tf_op jit(solution)/shard_map/while/body/eval_jaxpr/gk,kbf->gbf/dot_general | solution.py:40
  84.5 4.7 %fusion.82 = f32[32,128,256]{2,1,0:T(8,128)} fusion(bf16[32,128,256]{2,0,1:T(8,128)(2,1)S(1)} %fusion.81, bf16[3,32,128,128]{3,2,1,0:T(8,128)(2,1)} %get-tuple-element.304, s32[]{:T(128)} %get-tuple-element.291), kind=kOutput, calls=%fused_computation.3.clone.1 | convolution fusion | flops 268435456 | bytes 7340544 | tf_op jit(solution)/shard_map/while/body/eval_jaxpr/gab,gbf->gaf/dot_general | solution.py:44
  89.2 6.8 %fusion.84 = f32[8,128,256]{2,0,1:T(8,128)S(1)} fusion(f32[32,128,256]{2,1,0:T(8,128)} %fusion.82, f32[8,128,256]{2,0,1:T(8,128)S(1)} %get-tuple-element.292, pred[]{:T(512)S(6)} %compare.6, f32[32]{0:T(128)S(1)} %fusion.83, s32[32]{0:T(128)S(1)} %get-tuple-element.245), kind=kOutput, calls=%fused_computation.4.clone.1 | convolution fusion | flops 101188096 | bytes 6291713 | tf_op jit(solution)/shard_map/while/body/eval_jaxpr/gk,gaf->kaf/dot_general | solution.py:54
  96.0 2.1 %fusion.81 = bf16[32,128,256]{2,0,1:T(8,128)(2,1)S(1)} fusion(bf16[16,128,256]{2,1,0:T(8,128)(2,1)} %get-tuple-element.306, s32[32]{0:T(128)S(1)} %get-tuple-element.244), kind=kOutput, calls=%fused_computation.6.clone.1 | convolution fusion | flops 33554944 | bytes 3145856 | tf_op jit(solution)/shard_map/while/body/eval_jaxpr/gk,kbf->gbf/dot_general | solution.py:40
  98.1 4.7 %fusion.82 = f32[32,128,256]{2,1,0:T(8,128)} fusion(bf16[32,128,256]{2,0,1:T(8,128)(2,1)S(1)} %fusion.81, bf16[3,32,128,128]{3,2,1,0:T(8,128)(2,1)} %get-tuple-element.304, s32[]{:T(128)} %get-tuple-element.291), kind=kOutput, calls=%fused_computation.3.clone.1 | convolution fusion | flops 268435456 | bytes 7340544 | tf_op jit(solution)/shard_map/while/body/eval_jaxpr/gab,gbf->gaf/dot_general | solution.py:44
  102.9 6.8 %fusion.84 = f32[8,128,256]{2,0,1:T(8,128)S(1)} fusion(f32[32,128,256]{2,1,0:T(8,128)} %fusion.82, f32[8,128,256]{2,0,1:T(8,128)S(1)} %get-tuple-element.292, pred[]{:T(512)S(6)} %compare.6, f32[32]{0:T(128)S(1)} %fusion.83, s32[32]{0:T(128)S(1)} %get-tuple-element.245), kind=kOutput, calls=%fused_computation.4.clone.1 | convolution fusion | flops 101188096 | bytes 6291713 | tf_op jit(solution)/shard_map/while/body/eval_jaxpr/gk,gaf->kaf/dot_general | solution.py:54
  109.7 0.0 copy-start.1
  109.7 0.0 copy-start.2
  109.7 0.0 copy-start.3
  109.7 0.0 copy-start.4
  109.7 1.3 copy.10
  111.0 0.0 reduce-scatter.3.cloned.1.call-update
  111.0 0.0 reduce-scatter.5.cloned.1.call-done
  111.1 30.0 %reduce-scatter.3.cloned.1.call-done = f32[256,256]{1,0:T(8,128)} async-done(((f32[1024,256]{1,0:T(8,128)}), f32[256,256]{1,0:T(8,128)}) %reduce-scatter.3.cloned.1.call-update) | async-done | bytes 262160 | tf_op jit(solution)/shard_map/reduce_scatter | solution.py:20
  141.1 0.0 copy-done
  141.1 0.0 copy-done.1
  141.1 0.0 copy-done.2
  141.1 0.0 copy-done.3
  141.1 0.0 copy-done.4
  141.1 2.2 %fusion.49 = bf16[256,256]{1,0:T(8,128)(2,1)} fusion(bf16[1024,256]{1,0:T(8,128)(2,1)S(1)} %copy-done, bf16[256,1024]{1,0:T(8,128)(2,1)S(1)} %copy-done.2, f32[1024]{0:T(1024)S(1)} %copy-done.3, f32[256,256]{1,0:T(8,128)} %reduce-scatter.5.cloned.1.call-done, f32[256,256]{1,0:T(8,128)} %reduce-scatter.3.cloned.1.call-done, ...), kind=kOutput, calls=%fused_computation.57 | convolution fusion | flops 269615104 | bytes 1840128 | tf_op jit(solution)/shard_map/dot_general | solution.py:104
  (15 shorter events, 0.1 us)
Async XLA Ops:
  6.5 134.5 %copy-start = (bf16[1024,256]{1,0:T(8,128)(2,1)S(1)}, bf16[1024,256]{1,0:T(8,128)(2,1)}, u32[]{:S(2)}) copy-start(bf16[1024,256]{1,0:T(8,128)(2,1)} %param.20) | copy-start | bytes 1572868
  6.5 62.2 %all-gather.2.cloned.1.call-start = ((), (), s32[]{:S(2)}) async-start(), calls=%async_computation.2 | async-start | bytes 1179648 | tf_op jit(solution)/shard_map/all_gather | solution.py:16
  7.3 103.8 %reduce-scatter.5.cloned.1.call-start = ((), (), s32[]{:S(2)}) async-start(), calls=%async_computation.4 | async-start | bytes 2359296 | tf_op jit(solution)/shard_map/reduce_scatter | solution.py:24
  68.4 72.6 %reduce-scatter.3.cloned.1.call-start = ((), (), s32[]{:S(2)}) async-start(), calls=%async_computation.3 | async-start | bytes 1310720 | tf_op jit(solution)/shard_map/reduce_scatter | solution.py:20
  109.7 31.4 %copy-start.1 = (bf16[256,256]{1,0:T(8,128)(2,1)S(1)}, bf16[256,256]{1,0:T(8,128)(2,1)}, u32[]{:S(2)}) copy-start(bf16[256,256]{1,0:T(8,128)(2,1)} %param.13) | copy-start | bytes 393220
  109.7 31.4 %copy-start.2 = (bf16[256,1024]{1,0:T(8,128)(2,1)S(1)}, bf16[256,1024]{1,0:T(8,128)(2,1)}, u32[]{:S(2)}) copy-start(bf16[256,1024]{1,0:T(8,128)(2,1)} %param.18) | copy-start | bytes 1572868
  109.7 31.4 %copy-start.3 = (f32[1024]{0:T(1024)S(1)}, f32[1024]{0:T(1024)}, u32[]{:S(2)}) copy-start(f32[1024]{0:T(1024)} %param.19) | copy-start | bytes 12292
  109.7 31.4 %copy-start.4 = (f32[256]{0:T(256)S(1)}, f32[256]{0:T(256)}, u32[]{:S(2)}) copy-start(f32[256]{0:T(256)} %param.21) | copy-start | bytes 3076
Sparse Core Ops, SparseCore 0:
  9.2 23.7 all-gather.1
  68.5 41.9 reduce-scatter.4
  113.0 28.0 reduce-scatter.2
where the time goes:
time: 152 us; the launch traced here: 150 us
  matrix products  81.2 us (53%)
  waiting for transfers between devices  30.8 us (20%)
  blocking collectives  16.1 us (11%)
  between operations  13.9 us (9%)
  local copies, waits for them, and re-layouts  4.69 us (3%)
  other arithmetic  2.73 us (2%)
    dot_general x6, matrix products, one_group(): jnp.einsum('gk,gaf->kaf', target_hot, contrib, precision=lax.Precision.HI...  41.6 us
    reduce_scatter x1, waiting for transfers between devices, reduce_rows(): lax.psum_scatter(partial_value, 'col', scatter_dimension=0, tiled=True)  30 us
    all_gather x1, blocking collectives, gather_rows(): return lax.all_gather(features, 'col', axis=0, tiled=True)  16.1 us
    dot_general x3, matrix products, one_group(): jnp.einsum('gab,gaf->gbf', tile_block, picked, preferred_element_type=jnp...  14.7 us
    dot_general x3, matrix products, one_group(): jnp.einsum('gab,gbf->gaf', tile_block, picked, preferred_element_type=jnp...  14.2 us
    dot_general x6, matrix products, one_group(): jnp.einsum('gk,kbf->gbf', source_hot, panel_blocks, preferred_element_typ...  8.48 us
    while x2, local copies, waits for them, and re-layouts, accumulate(): totals, _ = lax.scan(one_group, starts, tuple(scanned))  3.83 us
  transfers between devices with their start and end apart: 3, of which 1 were waited for; matrix products, arithmetic and copies ran while one was open for 58% of the time, Pallas kernels for 0%

commit v1 on v0

v1 whole, which is shorter than its diff:
```python
import functools

import jax
import jax.numpy as jnp
from jax import lax
from jax.experimental import pallas as pl
from jax.experimental.pallas import tpu as pltpu
from jax.sharding import PartitionSpec as P

TILE = 128
CORES = 2
CHUNKS = 2
MESH = pl.DeviceIdType.MESH


def both(*conditions):
    result = conditions[0]
    for condition in conditions[1:]:
        result = jnp.logical_and(result, condition)
    return result


def kernel(
    n_row,
    n_col,
    x_ref,
    adjacency_ref,
    tile_row_ref,
    tile_column_ref,
    count_ref,
    weight_in_ref,
    bias_in_ref,
    weight_out_ref,
    bias_out_ref,
    out_ref,
    adj,
    dense,
    keys,
    slots_v,
    slots,
    w_in,
    w_out,
    xcol,
    xrow,
    acc_r,
    acc_c,
    row_send,
    row_up,
    row_down,
    sib_send,
    sib_recv,
    col_send,
    col_recv,
    combined,
    local_sem,
    gather_up_sem,
    gather_down_sem,
    gather_recv_sem,
    plane_send_sem,
    plane_recv_sem,
    sibling_send_sem,
    up_send_sem,
    up_recv_sem,
    down_send_sem,
    down_recv_sem,
    pair_send_sem,
    pair_recv_sem,
    col_send_sem,
    col_recv_sem,
):
    chunks, _, fw, rows = xrow.shape
    blocks = rows // TILE
    cap = adjacency_ref.shape[1]
    row_blocks = n_col * blocks
    col_blocks = n_row * blocks
    places = row_blocks * col_blocks
    chips = n_row // CORES
    r = lax.axis_index("row")
    c = lax.axis_index("col")
    k = r // CORES
    q = r % CORES
    other = 1 - q
    sibling = (k * CORES + other, c)
    above = (r, c + 1)
    below = (r, c - 1)
    pending = []

    def send(condition, make):
        @pl.when(condition)
        def _():
            make().start()

        pending.append((condition, make))

    def remote(src, dst, send_sem, recv_sem, device):
        return pltpu.make_async_remote_copy(
            src_ref=src,
            dst_ref=dst,
            send_sem=send_sem,
            recv_sem=recv_sem,
            device_id=device,
            device_id_type=MESH,
        )

    def arrived(dst, sem):
        pltpu.make_async_copy(dst, dst, sem).wait()

    barrier = pltpu.get_barrier_semaphore()
    pl.semaphore_signal(barrier, inc=1, device_id=sibling, device_id_type=MESH)
    for kk in range(chips):

        @pl.when(k != kk)
        def _():
            pl.semaphore_signal(
                barrier, inc=1, device_id=(kk * CORES + q, c), device_id_type=MESH
            )

    @pl.when(c > 0)
    def _():
        pl.semaphore_signal(barrier, inc=1, device_id=below, device_id_type=MESH)

    @pl.when(c < n_col - 1)
    def _():
        pl.semaphore_signal(barrier, inc=1, device_id=above, device_id_type=MESH)

    adj_copy = pltpu.make_async_copy(
        adjacency_ref.at[0], adj.at[pl.ds(0, cap)], local_sem.at[0]
    )
    adj_copy.start()
    in_copy = pltpu.make_async_copy(weight_in_ref, w_in, local_sem.at[1])
    in_copy.start()
    out_copy = pltpu.make_async_copy(weight_out_ref, w_out, local_sem.at[2])
    out_copy.start()

    x = x_ref[...]
    xt = x.T
    for h in range(chunks):
        xcol[h, r] = x[:, h * fw : (h + 1) * fw]
        xrow[h, c] = xt[h * fw : (h + 1) * fw, :]

    has_below = (c + n_col - 1) // n_col
    has_above = (2 * n_col - 2 - c) // n_col
    pl.semaphore_wait(barrier, chips + has_below + has_above)

    def gather_send(h, b, up):
        device = above if up else below
        sem = gather_up_sem if up else gather_down_sem
        return remote(
            xrow.at[h, b], xrow.at[h, b], sem.at[h, b], gather_recv_sem.at[h, b], device
        )

    def gather_own(h):
        send(c < n_col - 1, functools.partial(gather_send, h, c, True))
        send(c > 0, functools.partial(gather_send, h, c, False))

    def sibling_send(h, b):
        return remote(
            xcol.at[h, b],
            xcol.at[h, b],
            sibling_send_sem.at[h, b],
            plane_recv_sem.at[h, b],
            sibling,
        )

    def plane_own(h):
        for kk in range(1, chips):
            send(
                kk > k,
                lambda kk=kk: remote(
                    xcol.at[h, r],
                    xcol.at[h, r],
                    plane_send_sem.at[h, kk],
                    plane_recv_sem.at[h, r],
                    (kk * CORES + q, c),
                ),
            )
        send(q == 0, functools.partial(sibling_send, h, r))

    gather_own(0)
    for h in range(chunks):
        plane_own(h)

    wide = keys.shape[1]
    keys[...] = jnp.full(keys.shape, -1, jnp.int32)
    slot_row = lax.broadcasted_iota(jnp.int32, (1, cap), 1)
    keys[0:1, 0:cap] = jnp.where(
        slot_row < count_ref[0],
        tile_row_ref[...] * col_blocks + tile_column_ref[...],
        -1,
    )
    key_column = jnp.broadcast_to(keys[0:1, :], (TILE, wide)).T[:, 0:1]
    hit = key_column == lax.broadcasted_iota(jnp.int32, (wide, places), 1)
    number = lax.broadcasted_iota(jnp.int32, (wide, places), 0)
    slots_v[...] = cap + jnp.sum(
        jnp.where(hit, number - cap, 0), axis=0, keepdims=True
    )
    slot_copy = pltpu.make_async_copy(slots_v, slots, local_sem.at[3])
    slot_copy.start()
    adj[cap] = jnp.zeros((TILE, TILE), jnp.bfloat16)
    slot_copy.wait()
    adj_copy.wait()

    @pl.loop(0, r + 1)
    def _(owner):
        for i in range(row_blocks):
            for b in range(blocks):
                place = i * col_blocks + owner * blocks + b
                dense[owner, pl.ds(i * TILE, TILE), pl.ds(b * TILE, TILE)] = adj[
                    slots[0, place]
                ]

    def to_rows(h, owner, first=False):
        added = jnp.dot(
            dense[owner], xcol[h, owner], preferred_element_type=jnp.float32
        ).reshape(n_col, rows, fw)
        if first:
            acc_r[h] = added
        else:
            acc_r[h] += added

    def to_cols(h, source, first=False):
        part = pl.ds(pl.multiple_of(source * rows, rows), rows)

        @pl.loop(0, r + 1)
        def _(owner):
            added = jnp.dot(
                xrow[h, source], dense[owner, part, :], preferred_element_type=jnp.float32
            )
            if first:
                acc_c[h, owner] = added
            else:
                acc_c[h, owner] += added

    def gather_step(h, s):
        @pl.when(c - s >= 0)
        def _():
            arrived(xrow.at[h, c - s], gather_recv_sem.at[h, c - s])

        send(both(c - s >= 0, c < n_col - 1), lambda: gather_send(h, c - s, True))

        @pl.when(c + s < n_col)
        def _():
            arrived(xrow.at[h, c + s], gather_recv_sem.at[h, c + s])

        send(both(c + s < n_col, c > 0), lambda: gather_send(h, c + s, False))

        if s == max(n_col - 2, 1) and h + 1 < chunks:
            gather_own(h + 1)

        @pl.when(c - s >= 0)
        def _():
            to_cols(h, c - s)

        @pl.when(c + s < n_col)
        def _():
            to_cols(h, c + s)

    def plane_step(h):
        for kk in reversed(range(chips - 1)):
            owner = kk * CORES + q

            @pl.when(kk < k)
            def _():
                arrived(xcol.at[h, owner], plane_recv_sem.at[h, owner])

            send(kk < k, functools.partial(sibling_send, h, owner))

            @pl.when(kk < k)
            def _():
                to_rows(h, owner)

        @pl.when(q == 1)
        def _():
            arrived(xcol.at[h, r - 1], plane_recv_sem.at[h, r - 1])
            to_rows(h, r - 1)

        for kk in reversed(range(chips - 1)):
            owner = kk * CORES + other

            @pl.when(kk < k)
            def _():
                arrived(xcol.at[h, owner], plane_recv_sem.at[h, owner])
                to_rows(h, owner)

    def reduce_rows(h, t):
        def one(d, ahead, first, last, landing, send_sem, recv_sem, device):
            @pl.when(both(ahead, first))
            def _():
                row_send[h, d] = acc_r[h, d].astype(jnp.bfloat16)

            @pl.when(both(ahead, jnp.logical_not(first)))
            def _():
                arrived(landing.at[h, d], recv_sem.at[h, d])
                row_send[h, d] = (
                    acc_r[h, d] + landing[h, d].astype(jnp.float32)
                ).astype(jnp.bfloat16)

            send(
                ahead,
                lambda: remote(
                    row_send.at[h, d],
                    landing.at[h, d],
                    send_sem.at[h, d],
                    recv_sem.at[h, d],
                    device,
                ),
            )

        up = n_col - 1 - t
        one(up, c < up, c == 0, None, row_up, up_send_sem, up_recv_sem, above)
        one(t, c > t, c == n_col - 1, None, row_down, down_send_sem, down_recv_sem, below)

    def pair_start(h):
        for kk in range(chips):
            condition = jnp.logical_or(kk < k, both(kk == k, q == 1))

            @pl.when(condition)
            def _():
                sib_send[h, kk] = acc_c[h, kk * CORES + other].astype(jnp.bfloat16)

            send(
                condition,
                lambda kk=kk: remote(
                    sib_send.at[h, kk],
                    sib_recv.at[h, kk],
                    pair_send_sem.at[h, kk],
                    pair_recv_sem.at[h, kk],
                    sibling,
                ),
            )

    def reduce_cols(h):
        for kk in range(chips - 1):

            @pl.when(kk < k)
            def _():
                arrived(sib_recv.at[h, kk], pair_recv_sem.at[h, kk])
                col_send[h, kk] = (
                    acc_c[h, kk * CORES + q] + sib_recv[h, kk].astype(jnp.float32)
                ).astype(jnp.bfloat16)

            send(
                kk < k,
                lambda kk=kk: remote(
                    col_send.at[h, kk],
                    col_recv.at[h, k],
                    col_send_sem.at[h, kk],
                    col_recv_sem.at[h, k],
                    (kk * CORES + q, c),
                ),
            )

    def finish(h):
        @pl.when(q == 0)
        def _():
            arrived(sib_recv.at[h, k], pair_recv_sem.at[h, k])
            acc_c[h, r] += sib_recv[h, k].astype(jnp.float32)

        for kk in range(1, chips):

            @pl.when(kk > k)
            def _():
                arrived(col_recv.at[h, kk], col_recv_sem.at[h, kk])
                acc_c[h, r] += col_recv[h, kk].astype(jnp.float32)

        @pl.when(c > 0)
        def _():
            arrived(row_up.at[h, c], up_recv_sem.at[h, c])
            acc_r[h, c] += row_up[h, c].astype(jnp.float32)

        @pl.when(c < n_col - 1)
        def _():
            arrived(row_down.at[h, c], down_recv_sem.at[h, c])
            acc_r[h, c] += row_down[h, c].astype(jnp.float32)

        combined[:, h * fw : (h + 1) * fw] = (
            xcol[h, r].astype(jnp.float32) + acc_r[h, c] + acc_c[h, r].T
        ).astype(jnp.bfloat16)

    for h in range(chunks):
        to_rows(h, r, True)
        to_cols(h, c, True)
    for h in range(chunks):
        gather_step(h, 1)
        if h > 0:
            reduce_cols(h - 1)
        plane_step(h)
        reduce_rows(h, 0)
        for s in range(2, n_col):
            gather_step(h, s)
            if s < n_col - 1:
                reduce_rows(h, s - 1)
        pair_start(h)
        reduce_rows(h, n_col - 2)
    reduce_cols(chunks - 1)
    in_copy.wait()
    out_copy.wait()
    for h in range(chunks):
        finish(h)

    hid = w_in.shape[1]
    part = min(hid, 256)
    total = jnp.zeros(out_ref.shape, jnp.float32) + bias_out_ref[...]
    for j in range(0, hid, part):
        hidden = jnp.dot(
            combined[...], w_in[:, j : j + part], preferred_element_type=jnp.float32
        )
        hidden = jnp.maximum(hidden + bias_in_ref[:, j : j + part], 0.0)
        total += jnp.dot(
            hidden.astype(jnp.bfloat16),
            w_out[j : j + part, :],
            preferred_element_type=jnp.float32,
        )
    out_ref[...] = total.astype(jnp.bfloat16)

    for condition, make in pending:

        @pl.when(condition)
        def _():
            make().wait_send()


def solution(mesh):
    n_row = mesh.shape["row"]
    n_col = mesh.shape["col"]
    chips = n_row // CORES

    def shards(
        features, adjacency, tile_row, tile_column, tile_count, weight_in, bias_in, weight_out, bias_out
    ):
        rows, width = features.shape
        cap = adjacency.shape[1]
        blocks = rows // TILE
        places = n_row * n_col * blocks * blocks
        fw = width // CHUNKS
        bf16, f32 = jnp.bfloat16, jnp.float32
        dma = pltpu.SemaphoreType.DMA
        vmem = pl.BlockSpec(memory_space=pltpu.VMEM)
        anywhere = pl.BlockSpec(memory_space=pl.ANY)
        scratch = [
            pltpu.VMEM((cap + 1, TILE, TILE), bf16),
            pltpu.VMEM((n_row, n_col * rows, rows), bf16),
            pltpu.VMEM((8, -(-cap // TILE) * TILE), jnp.int32),
            pltpu.VMEM((1, places), jnp.int32),
            pltpu.SMEM((1, places), jnp.int32),
            pltpu.VMEM(weight_in.shape, bf16),
            pltpu.VMEM(weight_out.shape, bf16),
            pltpu.VMEM((CHUNKS, n_row, rows, fw), bf16),
            pltpu.VMEM((CHUNKS, n_col, fw, rows), bf16),
            pltpu.VMEM((CHUNKS, n_col, rows, fw), f32),
            pltpu.VMEM((CHUNKS, n_row, fw, rows), f32),
            pltpu.VMEM((CHUNKS, n_col, rows, fw), bf16),
            pltpu.VMEM((CHUNKS, n_col, rows, fw), bf16),
            pltpu.VMEM((CHUNKS, n_col, rows, fw), bf16),
            pltpu.VMEM((CHUNKS, chips, fw, rows), bf16),
            pltpu.VMEM((CHUNKS, chips, fw, rows), bf16),
            pltpu.VMEM((CHUNKS, chips, fw, rows), bf16),
            pltpu.VMEM((CHUNKS, chips, fw, rows), bf16),
            pltpu.VMEM((rows, width), bf16),
            dma((4,)),
            dma((CHUNKS, n_col)),
            dma((CHUNKS, n_col)),
            dma((CHUNKS, n_col)),
            dma((CHUNKS, chips)),
            dma((CHUNKS, n_row)),
            dma((CHUNKS, n_row)),
            dma((CHUNKS, n_col)),
            dma((CHUNKS, n_col)),
            dma((CHUNKS, n_col)),
            dma((CHUNKS, n_col)),
            dma((CHUNKS, chips)),
            dma((CHUNKS, chips)),
            dma((CHUNKS, chips)),
            dma((CHUNKS, chips)),
        ]
        return pl.pallas_call(
            functools.partial(kernel, n_row, n_col),
            out_shape=jax.ShapeDtypeStruct((rows, width), bf16),
            in_specs=[
                vmem,
                anywhere,
                vmem,
                vmem,
                pl.BlockSpec(memory_space=pltpu.SMEM),
                anywhere,
                vmem,
                anywhere,
                vmem,
            ],
            out_specs=vmem,
            scratch_shapes=scratch,
            compiler_params=pltpu.CompilerParams(
                collective_id=0, has_side_effects=True, vmem_limit_bytes=56 * 1024 * 1024
            ),
            name="gin_layer",
        )(
            features,
            adjacency,
            tile_row,
            tile_column,
            tile_count,
            weight_in,
            bias_in.reshape(1, -1),
            weight_out,
            bias_out.reshape(1, -1),
        )

    placed = (
        P(("row", "col"), None),
        P(("row", "col"), None, None, None),
        P(("row", "col"), None),
        P(("row", "col"), None),
        P(("row", "col")),
        P(),
        P(),
        P(),
        P(),
    )
    return jax.shard_map(
        shards, mesh=mesh, in_specs=placed, out_specs=P(("row", "col"), None), check_vma=False
    )
```

time: 152 us -> 56.9 us (0.37)
  the two profiles are of different devices: /device:TPU:6 before, /device:TPU:1 now
where the time goes in v1:
time: 56.9 us; the launch traced here: 56.7 us
  Pallas kernels  54.5 us (96%)
  local copies, waits for them, and re-layouts  1.57 us (3%)
  between operations  0.66 us (1%)
    pallas_call x1, Pallas kernels, shards(): pl.pallas_call(functools.partial(kernel, n_row, n_col), out_shape=jax.Sha...  54.5 us
    unnamed x1, local copies, waits for them, and re-layouts  1.57 us

profile of v1, /device:TPU:1, one launch (start us, length us, event | category | flops | bytes accessed | tf_op | source)
XLA Modules:
  0.0 56.7 jit_solution(18201388287888390749)
XLA Ops:
  0.7 54.5 %gin_layer.1 = bf16[256,256]{1,0:T(8,128)(2,1)} custom-call(bf16[256,256]{1,0:T(8,128)(2,1)} %x_ref.1, bf16[1,96,128,128]{3,2,1,0:T(8,128)(2,1)} %adjacency_ref.1, s32[1,96]{1,0:T(1,128)} %tile_row_ref.1, s32[1,96]{1,0:T(1,128)} %tile_column_ref.1, s32[1]{0:T(128)S(6)} %copy.11.count_ref, bf16[256,1024]{1,0:T(8,128)(2,1)} %weight_in_ref.1, ...), custom_call_target="tpu_custom_call" | custom-call | tf_op jit(solution)/shard_map/gin_layer/pallas_call | solution.py:476
  55.2 1.6 %copy.12 = bf16[256,256]{1,0:T(8,128)(2,1)} copy(bf16[256,256]{1,0:T(8,128)(2,1)} %gin_layer.1) | data formatting | bytes 262144

commit v2 on v1

v2 whole, which is shorter than its diff:
```python
import functools

import jax
import jax.numpy as jnp
from jax import lax
from jax.experimental import pallas as pl
from jax.experimental.pallas import tpu as pltpu
from jax.sharding import PartitionSpec as P

TILE = 128
CORES = 2
MESH = pl.DeviceIdType.MESH


def both(*conditions):
    result = conditions[0]
    for condition in conditions[1:]:
        result = jnp.logical_and(result, condition)
    return result


def kernel(
    n_row,
    n_col,
    x_ref,
    adjacency_ref,
    tile_row_ref,
    tile_column_ref,
    count_ref,
    weight_in_ref,
    bias_in_ref,
    weight_out_ref,
    bias_out_ref,
    out_ref,
    adj,
    dense,
    keys,
    slots_v,
    slots,
    w_in,
    w_out,
    xcol,
    xrow,
    acc_r,
    acc_c,
    row_send,
    row_up,
    row_down,
    sib_send,
    sib_recv,
    col_send,
    col_recv,
    local_sem,
    gather_up_sem,
    gather_down_sem,
    gather_recv_sem,
    plane_send_sem,
    plane_recv_sem,
    sibling_send_sem,
    up_send_sem,
    up_recv_sem,
    down_send_sem,
    down_recv_sem,
    pair_send_sem,
    pair_recv_sem,
    col_send_sem,
    col_recv_sem,
):
    _, width, rows = xrow.shape
    blocks = rows // TILE
    cap = adjacency_ref.shape[1]
    row_blocks = n_col * blocks
    col_blocks = n_row * blocks
    places = row_blocks * col_blocks
    chips = n_row // CORES
    wide = CORES * rows
    r = lax.axis_index("row")
    c = lax.axis_index("col")
    k = r // CORES
    q = r % CORES
    other = 1 - q
    sibling = (k * CORES + other, c)
    above = (r, c + 1)
    below = (r, c - 1)
    f32, bf16 = jnp.float32, jnp.bfloat16

    def remote(src, dst, send_sem, recv_sem, device):
        return pltpu.make_async_remote_copy(
            src_ref=src,
            dst_ref=dst,
            send_sem=send_sem,
            recv_sem=recv_sem,
            device_id=device,
            device_id_type=MESH,
        )

    def arrived(dst, sem):
        pltpu.make_async_copy(dst, dst, sem).wait()

    def run(condition, make, start):
        @pl.when(condition)
        def _():
            if start:
                make().start()
            else:
                make().wait_send()

    def gather_copy(b, up):
        sem = gather_up_sem if up else gather_down_sem
        device = above if up else below
        return remote(xrow.at[b], xrow.at[b], sem.at[b], gather_recv_sem.at[b], device)

    def gather_up(b, start):
        run(both(b >= 0, c < n_col - 1), lambda: gather_copy(b, True), start)

    def gather_down(b, start):
        run(both(b < n_col, c > 0), lambda: gather_copy(b, False), start)

    def plane(kk, start):
        run(
            kk > k,
            lambda: remote(
                xcol.at[k, pl.ds(q * rows, rows)],
                xcol.at[k, pl.ds(q * rows, rows)],
                plane_send_sem.at[kk],
                plane_recv_sem.at[r],
                (kk * CORES + q, c),
            ),
            start,
        )

    def to_sibling(kk, start):
        run(
            jnp.logical_or(kk < k, q == 0),
            lambda: remote(
                xcol.at[kk, pl.ds(q * rows, rows)],
                xcol.at[kk, pl.ds(q * rows, rows)],
                sibling_send_sem.at[kk],
                plane_recv_sem.at[kk * CORES + q],
                sibling,
            ),
            start,
        )

    def row_sum(d, up, start):
        run(
            c < d if up else c > d,
            lambda: remote(
                row_send.at[d],
                (row_up if up else row_down).at[d],
                (up_send_sem if up else down_send_sem).at[d],
                (up_recv_sem if up else down_recv_sem).at[d],
                above if up else below,
            ),
            start,
        )

    def pair(kk, start):
        run(
            jnp.logical_or(kk < k, q == 1),
            lambda: remote(
                sib_send.at[kk],
                sib_recv.at[kk],
                pair_send_sem.at[kk],
                pair_recv_sem.at[kk],
                sibling,
            ),
            start,
        )

    def col_sum(kk):
        return remote(
            col_send.at[kk],
            col_recv.at[k],
            col_send_sem.at[kk],
            col_recv_sem.at[k],
            (kk * CORES + q, c),
        )

    barrier = pltpu.get_barrier_semaphore()
    pl.semaphore_signal(barrier, inc=1, device_id=sibling, device_id_type=MESH)
    for kk in range(chips):

        @pl.when(k != kk)
        def _():
            pl.semaphore_signal(
                barrier, inc=1, device_id=(kk * CORES + q, c), device_id_type=MESH
            )

    @pl.when(c > 0)
    def _():
        pl.semaphore_signal(barrier, inc=1, device_id=below, device_id_type=MESH)

    @pl.when(c < n_col - 1)
    def _():
        pl.semaphore_signal(barrier, inc=1, device_id=above, device_id_type=MESH)

    adj_copy = pltpu.make_async_copy(
        adjacency_ref.at[0], adj.at[pl.ds(0, cap)], local_sem.at[0]
    )
    adj_copy.start()
    in_copy = pltpu.make_async_copy(weight_in_ref, w_in, local_sem.at[1])
    in_copy.start()
    out_copy = pltpu.make_async_copy(weight_out_ref, w_out, local_sem.at[2])
    out_copy.start()

    xcol[k, pl.ds(pl.multiple_of(q * rows, rows), rows)] = x_ref[...]
    xrow[c] = x_ref[...].T

    lanes = keys.shape[1]
    keys[...] = jnp.full(keys.shape, -1, jnp.int32)
    slot_row = lax.broadcasted_iota(jnp.int32, (1, cap), 1)
    keys[0:1, 0:cap] = jnp.where(
        slot_row < count_ref[0],
        tile_row_ref[...] * col_blocks + tile_column_ref[...],
        -1,
    )
    key_column = jnp.broadcast_to(keys[0:1, :], (TILE, lanes)).T[:, 0:1]
    hit = key_column == lax.broadcasted_iota(jnp.int32, (lanes, places), 1)
    number = lax.broadcasted_iota(jnp.int32, (lanes, places), 0)
    slots_v[...] = cap + jnp.sum(
        jnp.where(hit, number - cap, 0), axis=0, keepdims=True
    )
    slot_copy = pltpu.make_async_copy(slots_v, slots, local_sem.at[3])
    slot_copy.start()
    adj[cap] = jnp.zeros((TILE, TILE), bf16)

    has_below = (c + n_col - 1) // n_col
    has_above = (2 * n_col - 2 - c) // n_col
    pl.semaphore_wait(barrier, chips + has_below + has_above)

    gather_up(c, True)
    gather_down(c, True)
    to_sibling(k, True)
    for kk in range(1, chips):
        plane(kk, True)

    @pl.when(q == 0)
    def _():
        xcol[k, pl.ds(rows, rows)] = jnp.zeros((rows, width), bf16)

    acc_r[...] = jnp.zeros(acc_r.shape, f32)
    acc_c[...] = jnp.zeros(acc_c.shape, f32)
    slot_copy.wait()
    adj_copy.wait()

    @pl.loop(0, chips)
    def _(kk):
        for i in range(row_blocks):
            for b in range(CORES * blocks):
                place = i * col_blocks + kk * (CORES * blocks) + b
                dense[kk, pl.ds(i * TILE, TILE), pl.ds(b * TILE, TILE)] = adj[
                    slots[0, place]
                ]

    def to_cols(source):
        part = pl.ds(pl.multiple_of(source * rows, rows), rows)
        for kk in range(chips):
            acc_c[kk] += jnp.dot(
                xrow[source], dense[kk, part, :], preferred_element_type=f32
            )

    def all_to_rows():
        @pl.loop(0, k + 1)
        def _(j):
            kk = k - j
            mine = xcol.at[kk, pl.ds(q * rows, rows)]
            theirs = xcol.at[kk, pl.ds(other * rows, rows)]

            @pl.when(j > 0)
            def _():
                arrived(mine, plane_recv_sem.at[kk * CORES + q])
                to_sibling(kk, True)

            @pl.when(jnp.logical_or(j > 0, q == 1))
            def _():
                arrived(theirs, plane_recv_sem.at[kk * CORES + other])

            acc_r[...] += jnp.dot(dense[kk], xcol[kk], preferred_element_type=f32).reshape(
                acc_r.shape
            )

    def reduce_rows(t):
        def one(d, up, ahead, first, landing, recv_sem):
            @pl.when(both(ahead, first))
            def _():
                row_send[d] = acc_r[d].astype(bf16)

            @pl.when(both(ahead, jnp.logical_not(first)))
            def _():
                arrived(landing.at[d], recv_sem.at[d])
                row_send[d] = (acc_r[d] + landing[d].astype(f32)).astype(bf16)

            row_sum(d, up, True)

        up = n_col - 1 - t
        one(up, True, c < up, c == 0, row_up, up_recv_sem)
        one(t, False, c > t, c == n_col - 1, row_down, down_recv_sem)

    to_cols(c)

    @pl.loop(1, n_col)
    def _(s):
        low, high = c - s, c + s

        @pl.when(low >= 0)
        def _():
            arrived(xrow.at[low], gather_recv_sem.at[low])

        gather_up(low, True)

        @pl.when(high < n_col)
        def _():
            arrived(xrow.at[high], gather_recv_sem.at[high])

        gather_down(high, True)

        @pl.when(s == 1)
        def _():
            all_to_rows()

        @pl.loop(0, 2)
        def _(u):
            source = low + 2 * s * u

            @pl.when(both(source >= 0, source < n_col))
            def _():
                to_cols(source)

        @pl.when(s < n_col - 1)
        def _():
            reduce_rows(s - 1)

    here = pl.ds(pl.multiple_of(q * rows, rows), rows)
    there = pl.ds(pl.multiple_of(other * rows, rows), rows)

    @pl.loop(0, k + 1)
    def _(kk):
        sib_send[kk] = acc_c[kk, :, there].astype(bf16)
        pair(kk, True)

    reduce_rows(n_col - 2)

    @pl.loop(0, k)
    def _(kk):
        arrived(sib_recv.at[kk], pair_recv_sem.at[kk])
        col_send[kk] = (acc_c[kk, :, here] + sib_recv[kk].astype(f32)).astype(bf16)
        col_sum(kk).start()

    in_copy.wait()
    out_copy.wait()

    @pl.when(q == 0)
    def _():
        arrived(sib_recv.at[k], pair_recv_sem.at[k])
        acc_c[k, :, here] += sib_recv[k].astype(f32)

    @pl.when(c > 0)
    def _():
        arrived(row_up.at[c], up_recv_sem.at[c])
        acc_r[c] += row_up[c].astype(f32)

    @pl.when(c < n_col - 1)
    def _():
        arrived(row_down.at[c], down_recv_sem.at[c])
        acc_r[c] += row_down[c].astype(f32)

    @pl.loop(k + 1, chips)
    def _(kk):
        arrived(col_recv.at[kk], col_recv_sem.at[kk])
        acc_c[k, :, here] += col_recv[kk].astype(f32)

    combined = (x_ref[...].astype(f32) + acc_r[c] + acc_c[k, :, here].T).astype(bf16)
    hid = w_in.shape[1]
    part = min(hid, 256)
    total = jnp.zeros(out_ref.shape, f32) + bias_out_ref[...]
    for j in range(0, hid, part):
        hidden = jnp.dot(combined, w_in[:, j : j + part], preferred_element_type=f32)
        hidden = jnp.maximum(hidden + bias_in_ref[:, j : j + part], 0.0)
        total += jnp.dot(
            hidden.astype(bf16), w_out[j : j + part, :], preferred_element_type=f32
        )
    out_ref[...] = total.astype(bf16)

    gather_up(c, False)
    gather_down(c, False)
    to_sibling(k, False)
    for kk in range(1, chips):
        plane(kk, False)

    @pl.loop(1, n_col)
    def _(s):
        gather_up(c - s, False)
        gather_down(c + s, False)
        row_sum(n_col - s, True, False)
        row_sum(s - 1, False, False)

    @pl.loop(0, k)
    def _(kk):
        to_sibling(kk, False)
        pair(kk, False)
        col_sum(kk).wait_send()

    pair(k, False)


def solution(mesh):
    n_row = mesh.shape["row"]
    n_col = mesh.shape["col"]
    chips = n_row // CORES

    def shards(
        features, adjacency, tile_row, tile_column, tile_count, weight_in, bias_in, weight_out, bias_out
    ):
        rows, width = features.shape
        cap = adjacency.shape[1]
        blocks = rows // TILE
        places = n_row * n_col * blocks * blocks
        bf16, f32 = jnp.bfloat16, jnp.float32
        dma = pltpu.SemaphoreType.DMA
        vmem = pl.BlockSpec(memory_space=pltpu.VMEM)
        anywhere = pl.BlockSpec(memory_space=pl.ANY)
        scratch = [
            pltpu.VMEM((cap + 1, TILE, TILE), bf16),
            pltpu.VMEM((chips, n_col * rows, CORES * rows), bf16),
            pltpu.VMEM((8, -(-cap // TILE) * TILE), jnp.int32),
            pltpu.VMEM((1, places), jnp.int32),
            pltpu.SMEM((1, places), jnp.int32),
            pltpu.VMEM(weight_in.shape, bf16),
            pltpu.VMEM(weight_out.shape, bf16),
            pltpu.VMEM((chips, CORES * rows, width), bf16),
            pltpu.VMEM((n_col, width, rows), bf16),
            pltpu.VMEM((n_col, rows, width), f32),
            pltpu.VMEM((chips, width, CORES * rows), f32),
            pltpu.VMEM((n_col, rows, width), bf16),
            pltpu.VMEM((n_col, rows, width), bf16),
            pltpu.VMEM((n_col, rows, width), bf16),
            pltpu.VMEM((chips, width, rows), bf16),
            pltpu.VMEM((chips, width, rows), bf16),
            pltpu.VMEM((chips, width, rows), bf16),
            pltpu.VMEM((chips, width, rows), bf16),
            dma((4,)),
            dma((n_col,)),
            dma((n_col,)),
            dma((n_col,)),
            dma((chips,)),
            dma((n_row,)),
            dma((chips,)),
            dma((n_col,)),
            dma((n_col,)),
            dma((n_col,)),
            dma((n_col,)),
            dma((chips,)),
            dma((chips,)),
            dma((chips,)),
            dma((chips,)),
        ]
        return pl.pallas_call(
            functools.partial(kernel, n_row, n_col),
            out_shape=jax.ShapeDtypeStruct((rows, width), bf16),
            in_specs=[
                vmem,
                anywhere,
                vmem,
                vmem,
                pl.BlockSpec(memory_space=pltpu.SMEM),
                anywhere,
                vmem,
                anywhere,
                vmem,
            ],
            out_specs=vmem,
            scratch_shapes=scratch,
            compiler_params=pltpu.CompilerParams(
                collective_id=0, has_side_effects=True, vmem_limit_bytes=56 * 1024 * 1024
            ),
            name="gin_layer",
        )(
            features,
            adjacency,
            tile_row,
            tile_column,
            tile_count,
            weight_in,
            bias_in.reshape(1, -1),
            weight_out,
            bias_out.reshape(1, -1),
        )

    placed = (
        P(("row", "col"), None),
        P(("row", "col"), None, None, None),
        P(("row", "col"), None),
        P(("row", "col"), None),
        P(("row", "col")),
        P(),
        P(),
        P(),
        P(),
    )
    return jax.shard_map(
        shards, mesh=mesh, in_specs=placed, out_specs=P(("row", "col"), None), check_vma=False
    )
```

time: 56.9 us -> 47.4 us (0.83)
  the two profiles are of different devices: /device:TPU:1 before, /device:TPU:5 now
where the time goes in v2:
time: 47.4 us; the launch traced here: 47.2 us
  Pallas kernels  45 us (95%)
  local copies, waits for them, and re-layouts  1.57 us (3%)
  between operations  0.66 us (1%)
    pallas_call x1, Pallas kernels, shards(): pl.pallas_call(functools.partial(kernel, n_row, n_col), out_shape=jax.Sha...  45 us
    unnamed x1, local copies, waits for them, and re-layouts  1.57 us

profile of v2, /device:TPU:5, one launch (start us, length us, event | category | flops | bytes accessed | tf_op | source)
XLA Modules:
  0.0 47.2 jit_solution(419387310513283850)
XLA Ops:
  0.7 45.0 %gin_layer.1 = bf16[256,256]{1,0:T(8,128)(2,1)} custom-call(bf16[256,256]{1,0:T(8,128)(2,1)} %x_ref.1, bf16[1,96,128,128]{3,2,1,0:T(8,128)(2,1)} %adjacency_ref.1, s32[1,96]{1,0:T(1,128)} %tile_row_ref.1, s32[1,96]{1,0:T(1,128)} %tile_column_ref.1, s32[1]{0:T(128)S(6)} %copy.11.count_ref, bf16[256,1024]{1,0:T(8,128)(2,1)} %weight_in_ref.1, ...), custom_call_target="tpu_custom_call" | custom-call | tf_op jit(solution)/shard_map/gin_layer/pallas_call | solution.py:458
  45.6 1.6 %copy.12 = bf16[256,256]{1,0:T(8,128)(2,1)} copy(bf16[256,256]{1,0:T(8,128)(2,1)} %gin_layer.1) | data formatting | bytes 262144

commit v3 on v2

--- a/solution.py
+++ b/solution.py
@@ -144,7 +144,7 @@
 
     def row_sum(d, up, start):
         run(
-            c < d if up else c > d,
+            both(c < d, d < n_col) if up else both(c > d, d >= 0),
             lambda: remote(
                 row_send.at[d],
                 (row_up if up else row_down).at[d],
@@ -260,9 +260,9 @@
                 xrow[source], dense[kk, part, :], preferred_element_type=f32
             )
 
-    def all_to_rows():
-        @pl.loop(0, k + 1)
-        def _(j):
+    def rows_step(j):
+        @pl.when(j <= k)
+        def _():
             kk = k - j
             mine = xcol.at[kk, pl.ds(q * rows, rows)]
             theirs = xcol.at[kk, pl.ds(other * rows, rows)]
@@ -279,6 +279,30 @@
             acc_r[...] += jnp.dot(dense[kk], xcol[kk], preferred_element_type=f32).reshape(
                 acc_r.shape
             )
+
+    def gather_step(s):
+        low, high = c - s, c + s
+
+        @pl.when(low >= 0)
+        def _():
+            arrived(xrow.at[low], gather_recv_sem.at[low])
+
+        gather_up(low, True)
+
+        @pl.when(high < n_col)
+        def _():
+            arrived(xrow.at[high], gather_recv_sem.at[high])
+
+        gather_down(high, True)
+
+    def cols_step(s):
+        @pl.loop(0, 2)
+        def _(u):
+            source = c - s + 2 * s * u
+
+            @pl.when(both(source >= 0, source < n_col))
+            def _():
+                to_cols(source)
 
     def reduce_rows(t):
         def one(d, up, ahead, first, landing, recv_sem):
@@ -293,43 +317,29 @@
 
             row_sum(d, up, True)
 
-        up = n_col - 1 - t
-        one(up, True, c < up, c == 0, row_up, up_recv_sem)
-        one(t, False, c > t, c == n_col - 1, row_down, down_recv_sem)
+        up = n_col - 1 - t + c
+        down = t - (n_col - 1) + c
+        one(up, True, both(c < up, up < n_col), c == 0, row_up, up_recv_sem)
+        one(down, False, both(c > down, down >= 0), c == n_col - 1, row_down, down_recv_sem)
 
     to_cols(c)
 
-    @pl.loop(1, n_col)
+    @pl.loop(0, max(chips, n_col - 1))
+    def _(j):
+        rows_step(j)
+
+        @pl.when(j < n_col - 2)
+        def _():
+            gather_step(j + 1)
+
+    reduce_rows(0)
+
+    @pl.loop(1, n_col - 1)
     def _(s):
-        low, high = c - s, c + s
-
-        @pl.when(low >= 0)
-        def _():
-            arrived(xrow.at[low], gather_recv_sem.at[low])
-
-        gather_up(low, True)
-
-        @pl.when(high < n_col)
-        def _():
-            arrived(xrow.at[high], gather_recv_sem.at[high])
-
-        gather_down(high, True)
-
-        @pl.when(s == 1)
-        def _():
-            all_to_rows()
-
-        @pl.loop(0, 2)
-        def _(u):
-            source = low + 2 * s * u
-
-            @pl.when(both(source >= 0, source < n_col))
-            def _():
-                to_cols(source)
-
-        @pl.when(s < n_col - 1)
-        def _():
-            reduce_rows(s - 1)
+        cols_step(s)
+
+    gather_step(n_col - 1)
+    cols_step(n_col - 1)
 
     here = pl.ds(pl.multiple_of(q * rows, rows), rows)
     there = pl.ds(pl.multiple_of(other * rows, rows), rows)
@@ -338,14 +348,16 @@
     def _(kk):
         sib_send[kk] = acc_c[kk, :, there].astype(bf16)
         pair(kk, True)
-
-    reduce_rows(n_col - 2)
 
     @pl.loop(0, k)
     def _(kk):
         arrived(sib_recv.at[kk], pair_recv_sem.at[kk])
         col_send[kk] = (acc_c[kk, :, here] + sib_recv[kk].astype(f32)).astype(bf16)
         col_sum(kk).start()
+
+    @pl.loop(1, n_col - 1)
+    def _(t):
+        reduce_rows(t)
 
     in_copy.wait()
     out_copy.wait()

time: 47.4 us -> 32.8 us (0.69)
  the two profiles are of different devices: /device:TPU:5 before, /device:TPU:0 now
where the time goes in v3:
time: 32.8 us; the launch traced here: 32.6 us
  Pallas kernels  30.4 us (93%)
  local copies, waits for them, and re-layouts  1.57 us (5%)
  between operations  0.66 us (2%)
    pallas_call x1, Pallas kernels, shards(): pl.pallas_call(functools.partial(kernel, n_row, n_col), out_shape=jax.Sha...  30.4 us
    unnamed x1, local copies, waits for them, and re-layouts  1.57 us

profile of v3, /device:TPU:0, one launch (start us, length us, event | category | flops | bytes accessed | tf_op | source)
XLA Modules:
  0.0 32.6 jit_solution(7134301803066965494)
XLA Ops:
  0.7 30.4 %gin_layer.1 = bf16[256,256]{1,0:T(8,128)(2,1)} custom-call(bf16[256,256]{1,0:T(8,128)(2,1)} %x_ref.1, bf16[1,96,128,128]{3,2,1,0:T(8,128)(2,1)} %adjacency_ref.1, s32[1,96]{1,0:T(1,128)} %tile_row_ref.1, s32[1,96]{1,0:T(1,128)} %tile_column_ref.1, s32[1]{0:T(128)S(6)} %copy.11.count_ref, bf16[256,1024]{1,0:T(8,128)(2,1)} %weight_in_ref.1, ...), custom_call_target="tpu_custom_call" | custom-call | tf_op jit(solution)/shard_map/gin_layer/pallas_call | solution.py:470
  31.1 1.6 %copy.12 = bf16[256,256]{1,0:T(8,128)(2,1)} copy(bf16[256,256]{1,0:T(8,128)(2,1)} %gin_layer.1) | data formatting | bytes 262144

commit v4 on v3

v4 whole, which is shorter than its diff:
```python
import functools

import jax
import jax.numpy as jnp
from jax import lax
from jax.experimental import pallas as pl
from jax.experimental.pallas import tpu as pltpu
from jax.sharding import PartitionSpec as P

TILE = 128
CORES = 2
CHUNKS = 2
MESH = pl.DeviceIdType.MESH


def both(*conditions):
    result = conditions[0]
    for condition in conditions[1:]:
        result = jnp.logical_and(result, condition)
    return result


def kernel(
    n_row,
    n_col,
    x_ref,
    adjacency_ref,
    tile_row_ref,
    tile_column_ref,
    count_ref,
    weight_in_ref,
    bias_in_ref,
    weight_out_ref,
    bias_out_ref,
    out_ref,
    adj,
    dense,
    keys,
    slots_v,
    slots,
    w_in,
    w_out,
    xcol,
    xrow,
    acc_r,
    acc_c,
    row_send,
    row_up,
    row_down,
    sib_send,
    sib_recv,
    col_send,
    col_recv,
    combined_ref,
    local_sem,
    gather_up_sem,
    gather_down_sem,
    gather_recv_sem,
    plane_send_sem,
    plane_recv_sem,
    sibling_send_sem,
    up_send_sem,
    up_recv_sem,
    down_send_sem,
    down_recv_sem,
    pair_send_sem,
    pair_recv_sem,
    col_send_sem,
    col_recv_sem,
):
    chunks, _, fw, rows = xrow.shape
    blocks = rows // TILE
    cap = adjacency_ref.shape[1]
    row_blocks = n_col * blocks
    col_blocks = n_row * blocks
    places = row_blocks * col_blocks
    chips = n_row // CORES
    wide = CORES * rows
    r = lax.axis_index("row")
    c = lax.axis_index("col")
    k = r // CORES
    q = r % CORES
    other = 1 - q
    sibling = (k * CORES + other, c)
    above = (r, c + 1)
    below = (r, c - 1)
    f32, bf16 = jnp.float32, jnp.bfloat16

    def remote(src, dst, send_sem, recv_sem, device):
        return pltpu.make_async_remote_copy(
            src_ref=src,
            dst_ref=dst,
            send_sem=send_sem,
            recv_sem=recv_sem,
            device_id=device,
            device_id_type=MESH,
        )

    def arrived(dst, sem):
        pltpu.make_async_copy(dst, dst, sem).wait()

    def run(condition, make, start):
        @pl.when(condition)
        def _():
            if start:
                make().start()
            else:
                make().wait_send()

    def gather_copy(h, b, up):
        sem = gather_up_sem if up else gather_down_sem
        device = above if up else below
        return remote(xrow.at[h, b], xrow.at[h, b], sem.at[h, b], gather_recv_sem.at[h, b], device)

    def gather_up(h, b, start):
        run(both(b >= 0, c < n_col - 1), lambda: gather_copy(h, b, True), start)

    def gather_down(h, b, start):
        run(both(b < n_col, c > 0), lambda: gather_copy(h, b, False), start)

    def plane(h, kk, start):
        run(
            kk > k,
            lambda: remote(
                xcol.at[h, k, pl.ds(q * rows, rows)],
                xcol.at[h, k, pl.ds(q * rows, rows)],
                plane_send_sem.at[h, kk],
                plane_recv_sem.at[h, r],
                (kk * CORES + q, c),
            ),
            start,
        )

    def to_sibling(h, kk, start):
        run(
            jnp.logical_or(kk < k, q == 0),
            lambda: remote(
                xcol.at[h, kk, pl.ds(q * rows, rows)],
                xcol.at[h, kk, pl.ds(q * rows, rows)],
                sibling_send_sem.at[h, kk],
                plane_recv_sem.at[h, kk * CORES + q],
                sibling,
            ),
            start,
        )

    def row_sum(h, d, up, start):
        run(
            both(c < d, d < n_col) if up else both(c > d, d >= 0),
            lambda: remote(
                row_send.at[h, d],
                (row_up if up else row_down).at[h, d],
                (up_send_sem if up else down_send_sem).at[h, d],
                (up_recv_sem if up else down_recv_sem).at[h, d],
                above if up else below,
            ),
            start,
        )

    def pair(h, kk, start):
        run(
            jnp.logical_or(kk < k, q == 1),
            lambda: remote(
                sib_send.at[h, kk],
                sib_recv.at[h, kk],
                pair_send_sem.at[h, kk],
                pair_recv_sem.at[h, kk],
                sibling,
            ),
            start,
        )

    def col_sum(h, kk):
        return remote(
            col_send.at[h, kk],
            col_recv.at[h, k],
            col_send_sem.at[h, kk],
            col_recv_sem.at[h, k],
            (kk * CORES + q, c),
        )

    barrier = pltpu.get_barrier_semaphore()
    pl.semaphore_signal(barrier, inc=1, device_id=sibling, device_id_type=MESH)
    for kk in range(chips):

        @pl.when(k != kk)
        def _():
            pl.semaphore_signal(
                barrier, inc=1, device_id=(kk * CORES + q, c), device_id_type=MESH
            )

    @pl.when(c > 0)
    def _():
        pl.semaphore_signal(barrier, inc=1, device_id=below, device_id_type=MESH)

    @pl.when(c < n_col - 1)
    def _():
        pl.semaphore_signal(barrier, inc=1, device_id=above, device_id_type=MESH)

    adj_copy = pltpu.make_async_copy(
        adjacency_ref.at[0], adj.at[pl.ds(0, cap)], local_sem.at[0]
    )
    adj_copy.start()
    in_copy = pltpu.make_async_copy(weight_in_ref, w_in, local_sem.at[1])
    in_copy.start()
    out_copy = pltpu.make_async_copy(weight_out_ref, w_out, local_sem.at[2])
    out_copy.start()

    here = pl.ds(pl.multiple_of(q * rows, rows), rows)
    there = pl.ds(pl.multiple_of(other * rows, rows), rows)
    for h in range(chunks):
        own = x_ref[:, h * fw : (h + 1) * fw]
        xcol[h, k, here] = own
        xrow[h, c] = own.T

    has_below = (c + n_col - 1) // n_col
    has_above = (2 * n_col - 2 - c) // n_col
    pl.semaphore_wait(barrier, chips + has_below + has_above)

    for h in range(chunks):
        gather_up(h, c, True)
        gather_down(h, c, True)
        for kk in range(1, chips):
            plane(h, kk, True)
        to_sibling(h, k, True)

        @pl.when(q == 0)
        def _():
            xcol[h, k, pl.ds(rows, rows)] = jnp.zeros((rows, fw), bf16)

    lanes = keys.shape[1]
    keys[...] = jnp.full(keys.shape, -1, jnp.int32)
    slot_row = lax.broadcasted_iota(jnp.int32, (1, cap), 1)
    keys[0:1, 0:cap] = jnp.where(
        slot_row < count_ref[0],
        tile_row_ref[...] * col_blocks + tile_column_ref[...],
        -1,
    )
    key_column = jnp.broadcast_to(keys[0:1, :], (TILE, lanes)).T[:, 0:1]
    hit = key_column == lax.broadcasted_iota(jnp.int32, (lanes, places), 1)
    number = lax.broadcasted_iota(jnp.int32, (lanes, places), 0)
    slots_v[...] = cap + jnp.sum(
        jnp.where(hit, number - cap, 0), axis=0, keepdims=True
    )
    slot_copy = pltpu.make_async_copy(slots_v, slots, local_sem.at[3])
    slot_copy.start()
    adj[cap] = jnp.zeros((TILE, TILE), bf16)

    acc_r[...] = jnp.zeros(acc_r.shape, f32)
    acc_c[...] = jnp.zeros(acc_c.shape, f32)
    slot_copy.wait()
    adj_copy.wait()

    @pl.loop(0, chips)
    def _(kk):
        for i in range(row_blocks):
            for b in range(CORES * blocks):
                place = i * col_blocks + kk * (CORES * blocks) + b
                dense[kk, pl.ds(i * TILE, TILE), pl.ds(b * TILE, TILE)] = adj[
                    slots[0, place]
                ]

    def to_cols(h, source):
        part = pl.ds(pl.multiple_of(source * rows, rows), rows)
        for kk in range(chips):
            acc_c[h, kk] += jnp.dot(
                xrow[h, source], dense[kk, part, :], preferred_element_type=f32
            )

    def rows_step(h, j):
        @pl.when(j <= k)
        def _():
            kk = k - j
            mine = xcol.at[h, kk, pl.ds(q * rows, rows)]
            theirs = xcol.at[h, kk, pl.ds(other * rows, rows)]

            @pl.when(j > 0)
            def _():
                arrived(mine, plane_recv_sem.at[h, kk * CORES + q])
                to_sibling(h, kk, True)

            @pl.when(jnp.logical_or(j > 0, q == 1))
            def _():
                arrived(theirs, plane_recv_sem.at[h, kk * CORES + other])

            acc_r[h] += jnp.dot(
                dense[kk], xcol[h, kk], preferred_element_type=f32
            ).reshape(n_col, rows, fw)

    def gather_step(h, s):
        low, high = c - s, c + s

        @pl.when(low >= 0)
        def _():
            arrived(xrow.at[h, low], gather_recv_sem.at[h, low])

        gather_up(h, low, True)

        @pl.when(high < n_col)
        def _():
            arrived(xrow.at[h, high], gather_recv_sem.at[h, high])

        gather_down(h, high, True)

    def cols_step(h, s):
        @pl.loop(0, 2)
        def _(u):
            source = c - s + 2 * s * u

            @pl.when(both(source >= 0, source < n_col))
            def _():
                to_cols(h, source)

    def reduce_rows(h, t):
        def one(d, up, ahead, first, landing, recv_sem):
            @pl.when(both(ahead, first))
            def _():
                row_send[h, d] = acc_r[h, d].astype(bf16)

            @pl.when(both(ahead, jnp.logical_not(first)))
            def _():
                arrived(landing.at[h, d], recv_sem.at[h, d])
                row_send[h, d] = (acc_r[h, d] + landing[h, d].astype(f32)).astype(bf16)

            row_sum(h, d, up, True)

        up = n_col - 1 - t + c
        down = t - (n_col - 1) + c
        one(up, True, both(c < up, up < n_col), c == 0, row_up, up_recv_sem)
        one(down, False, both(c > down, down >= 0), c == n_col - 1, row_down, down_recv_sem)

    def pair_start(h):
        @pl.loop(0, k + 1)
        def _(kk):
            sib_send[h, kk] = acc_c[h, kk, :, there].astype(bf16)
            pair(h, kk, True)

    def reduce_cols(h):
        @pl.loop(0, k)
        def _(kk):
            arrived(sib_recv.at[h, kk], pair_recv_sem.at[h, kk])
            col_send[h, kk] = (
                acc_c[h, kk, :, here] + sib_recv[h, kk].astype(f32)
            ).astype(bf16)
            col_sum(h, kk).start()

    def finish(h):
        @pl.when(q == 0)
        def _():
            arrived(sib_recv.at[h, k], pair_recv_sem.at[h, k])
            acc_c[h, k, :, here] += sib_recv[h, k].astype(f32)

        @pl.loop(k + 1, chips)
        def _(kk):
            arrived(col_recv.at[h, kk], col_recv_sem.at[h, kk])
            acc_c[h, k, :, here] += col_recv[h, kk].astype(f32)

        @pl.when(c > 0)
        def _():
            arrived(row_up.at[h, c], up_recv_sem.at[h, c])
            acc_r[h, c] += row_up[h, c].astype(f32)

        @pl.when(c < n_col - 1)
        def _():
            arrived(row_down.at[h, c], down_recv_sem.at[h, c])
            acc_r[h, c] += row_down[h, c].astype(f32)

        own = x_ref[:, h * fw : (h + 1) * fw].astype(f32)
        combined_ref[:, h * fw : (h + 1) * fw] = (
            own + acc_r[h, c] + acc_c[h, k, :, here].T
        ).astype(bf16)

    last = n_col - 1
    for h in range(chunks):
        to_cols(h, c)
    for h in range(chunks):

        @pl.loop(0, max(chips, last))
        def _(j):
            rows_step(h, j)
            if h == 0:

                @pl.when(j < last - 1)
                def _():
                    for g in range(chunks):
                        gather_step(g, j + 1)

        reduce_rows(h, 0)
        if h == 0:

            @pl.loop(1, last)
            def _(s):
                cols_step(0, s)

    for h in range(chunks):
        if h > 0:

            @pl.loop(1, last)
            def _(s):
                cols_step(h, s)

        gather_step(h, last)
        cols_step(h, last)
        pair_start(h)
        reduce_rows(h, 1)
        if h < chunks - 1:
            reduce_cols(h)

    @pl.loop(2, last)
    def _(t):
        for h in range(chunks - 1):
            reduce_rows(h, t)

    reduce_cols(chunks - 1)

    @pl.loop(2, last)
    def _(t):
        reduce_rows(chunks - 1, t)

    in_copy.wait()
    out_copy.wait()
    for h in range(chunks):
        finish(h)

    combined = combined_ref[...]
    hid = w_in.shape[1]
    part = min(hid, 256)
    total = jnp.zeros(out_ref.shape, f32) + bias_out_ref[...]
    for j in range(0, hid, part):
        hidden = jnp.dot(combined, w_in[:, j : j + part], preferred_element_type=f32)
        hidden = jnp.maximum(hidden + bias_in_ref[:, j : j + part], 0.0)
        total += jnp.dot(
            hidden.astype(bf16), w_out[j : j + part, :], preferred_element_type=f32
        )
    out_ref[...] = total.astype(bf16)

    for h in range(chunks):
        gather_up(h, c, False)
        gather_down(h, c, False)
        to_sibling(h, k, False)
        for kk in range(1, chips):
            plane(h, kk, False)

        @pl.loop(1, n_col)
        def _(s):
            gather_up(h, c - s, False)
            gather_down(h, c + s, False)
            row_sum(h, n_col - s, True, False)
            row_sum(h, s - 1, False, False)

        @pl.loop(0, k)
        def _(kk):
            to_sibling(h, kk, False)
            pair(h, kk, False)
            col_sum(h, kk).wait_send()

        pair(h, k, False)


def solution(mesh):
    n_row = mesh.shape["row"]
    n_col = mesh.shape["col"]
    chips = n_row // CORES

    def shards(
        features, adjacency, tile_row, tile_column, tile_count, weight_in, bias_in, weight_out, bias_out
    ):
        rows, width = features.shape
        fw = width // CHUNKS
        cap = adjacency.shape[1]
        blocks = rows // TILE
        places = n_row * n_col * blocks * blocks
        bf16, f32 = jnp.bfloat16, jnp.float32
        dma = pltpu.SemaphoreType.DMA
        vmem = pl.BlockSpec(memory_space=pltpu.VMEM)
        anywhere = pl.BlockSpec(memory_space=pl.ANY)
        scratch = [
            pltpu.VMEM((cap + 1, TILE, TILE), bf16),
            pltpu.VMEM((chips, n_col * rows, CORES * rows), bf16),
            pltpu.VMEM((8, -(-cap // TILE) * TILE), jnp.int32),
            pltpu.VMEM((1, places), jnp.int32),
            pltpu.SMEM((1, places), jnp.int32),
            pltpu.VMEM(weight_in.shape, bf16),
            pltpu.VMEM(weight_out.shape, bf16),
            pltpu.VMEM((CHUNKS, chips, CORES * rows, fw), bf16),
            pltpu.VMEM((CHUNKS, n_col, fw, rows), bf16),
            pltpu.VMEM((CHUNKS, n_col, rows, fw), f32),
            pltpu.VMEM((CHUNKS, chips, fw, CORES * rows), f32),
            pltpu.VMEM((CHUNKS, n_col, rows, fw), bf16),
            pltpu.VMEM((CHUNKS, n_col, rows, fw), bf16),
            pltpu.VMEM((CHUNKS, n_col, rows, fw), bf16),
            pltpu.VMEM((CHUNKS, chips, fw, rows), bf16),
            pltpu.VMEM((CHUNKS, chips, fw, rows), bf16),
            pltpu.VMEM((CHUNKS, chips, fw, rows), bf16),
            pltpu.VMEM((CHUNKS, chips, fw, rows), bf16),
            pltpu.VMEM((rows, width), bf16),
            dma((4,)),
            dma((CHUNKS, n_col)),
            dma((CHUNKS, n_col)),
            dma((CHUNKS, n_col)),
            dma((CHUNKS, chips)),
            dma((CHUNKS, n_row)),
            dma((CHUNKS, chips)),
            dma((CHUNKS, n_col)),
            dma((CHUNKS, n_col)),
            dma((CHUNKS, n_col)),
            dma((CHUNKS, n_col)),
            dma((CHUNKS, chips)),
            dma((CHUNKS, chips)),
            dma((CHUNKS, chips)),
            dma((CHUNKS, chips)),
        ]
        return pl.pallas_call(
            functools.partial(kernel, n_row, n_col),
            out_shape=jax.ShapeDtypeStruct((rows, width), bf16),
            in_specs=[
                vmem,
                anywhere,
                vmem,
                vmem,
                pl.BlockSpec(memory_space=pltpu.SMEM),
                anywhere,
                vmem,
                anywhere,
                vmem,
            ],
            out_specs=vmem,
            scratch_shapes=scratch,
            compiler_params=pltpu.CompilerParams(
                collective_id=0, has_side_effects=True, vmem_limit_bytes=56 * 1024 * 1024
            ),
            name="gin_layer",
        )(
            features,
            adjacency,
            tile_row,
            tile_column,
            tile_count,
            weight_in,
            bias_in.reshape(1, -1),
            weight_out,
            bias_out.reshape(1, -1),
        )

    placed = (
        P(("row", "col"), None),
        P(("row", "col"), None, None, None),
        P(("row", "col"), None),
        P(("row", "col"), None),
        P(("row", "col")),
        P(),
        P(),
        P(),
        P(),
    )
    return jax.shard_map(
        shards, mesh=mesh, in_specs=placed, out_specs=P(("row", "col"), None), check_vma=False
    )
```

time: 32.8 us -> 34.7 us (1.058)
  the two profiles are of different devices: /device:TPU:0 before, /device:TPU:6 now
where the time goes in v4:
time: 34.7 us; the launch traced here: 34.6 us
  Pallas kernels  32.3 us (93%)
  local copies, waits for them, and re-layouts  1.57 us (5%)
  between operations  0.66 us (2%)
    pallas_call x1, Pallas kernels, shards(): pl.pallas_call(functools.partial(kernel, n_row, n_col), out_shape=jax.Sha...  32.3 us
    unnamed x1, local copies, waits for them, and re-layouts  1.57 us

profile of v4, /device:TPU:6, one launch (start us, length us, event | category | flops | bytes accessed | tf_op | source)
XLA Modules:
  0.0 34.6 jit_solution(1260626641284390247)
XLA Ops:
  0.7 32.3 %gin_layer.1 = bf16[256,256]{1,0:T(8,128)(2,1)} custom-call(bf16[256,256]{1,0:T(8,128)(2,1)} %x_ref.1, bf16[1,96,128,128]{3,2,1,0:T(8,128)(2,1)} %adjacency_ref.1, s32[1,96]{1,0:T(1,128)} %tile_row_ref.1, s32[1,96]{1,0:T(1,128)} %tile_column_ref.1, s32[1]{0:T(128)S(6)} %copy.11.count_ref, bf16[256,1024]{1,0:T(8,128)(2,1)} %weight_in_ref.1, ...), custom_call_target="tpu_custom_call" | custom-call | tf_op jit(solution)/shard_map/gin_layer/pallas_call | solution.py:513
  33.0 1.6 %copy.12 = bf16[256,256]{1,0:T(8,128)(2,1)} copy(bf16[256,256]{1,0:T(8,128)(2,1)} %gin_layer.1) | data formatting | bytes 262144

commit v5 on v3

--- a/solution.py
+++ b/solution.py
@@ -207,6 +207,20 @@
     xcol[k, pl.ds(pl.multiple_of(q * rows, rows), rows)] = x_ref[...]
     xrow[c] = x_ref[...].T
 
+    has_below = (c + n_col - 1) // n_col
+    has_above = (2 * n_col - 2 - c) // n_col
+    pl.semaphore_wait(barrier, chips + has_below + has_above)
+
+    gather_up(c, True)
+    gather_down(c, True)
+    to_sibling(k, True)
+    for kk in range(1, chips):
+        plane(kk, True)
+
+    @pl.when(q == 0)
+    def _():
+        xcol[k, pl.ds(rows, rows)] = jnp.zeros((rows, width), bf16)
+
     lanes = keys.shape[1]
     keys[...] = jnp.full(keys.shape, -1, jnp.int32)
     slot_row = lax.broadcasted_iota(jnp.int32, (1, cap), 1)
@@ -225,22 +239,6 @@
     slot_copy.start()
     adj[cap] = jnp.zeros((TILE, TILE), bf16)
 
-    has_below = (c + n_col - 1) // n_col
-    has_above = (2 * n_col - 2 - c) // n_col
-    pl.semaphore_wait(barrier, chips + has_below + has_above)
-
-    gather_up(c, True)
-    gather_down(c, True)
-    to_sibling(k, True)
-    for kk in range(1, chips):
-        plane(kk, True)
-
-    @pl.when(q == 0)
-    def _():
-        xcol[k, pl.ds(rows, rows)] = jnp.zeros((rows, width), bf16)
-
-    acc_r[...] = jnp.zeros(acc_r.shape, f32)
-    acc_c[...] = jnp.zeros(acc_c.shape, f32)
     slot_copy.wait()
     adj_copy.wait()
 
@@ -253,14 +251,13 @@
                     slots[0, place]
                 ]
 
-    def to_cols(source):
+    def to_cols(source, first=False):
         part = pl.ds(pl.multiple_of(source * rows, rows), rows)
         for kk in range(chips):
-            acc_c[kk] += jnp.dot(
-                xrow[source], dense[kk, part, :], preferred_element_type=f32
-            )
-
-    def rows_step(j):
+            added = jnp.dot(xrow[source], dense[kk, part, :], preferred_element_type=f32)
+            acc_c[kk] = added if first else acc_c[kk] + added
+
+    def rows_step(j, first=False):
         @pl.when(j <= k)
         def _():
             kk = k - j
@@ -276,9 +273,9 @@
             def _():
                 arrived(theirs, plane_recv_sem.at[kk * CORES + other])
 
-            acc_r[...] += jnp.dot(dense[kk], xcol[kk], preferred_element_type=f32).reshape(
-                acc_r.shape
-            )
+            added = jnp.dot(dense[kk], xcol[kk], preferred_element_type=f32)
+            added = added.reshape(acc_r.shape)
+            acc_r[...] = added if first else acc_r[...] + added
 
     def gather_step(s):
         low, high = c - s, c + s
@@ -304,27 +301,41 @@
             def _():
                 to_cols(source)
 
+    def start_rows():
+        @pl.when(c == 0)
+        def _():
+            @pl.loop(1, n_col)
+            def _(s):
+                row_send[n_col - s] = acc_r[n_col - s].astype(bf16)
+                row_sum(n_col - s, True, True)
+
+        @pl.when(c == n_col - 1)
+        def _():
+            @pl.loop(0, n_col - 1)
+            def _(d):
+                row_send[d] = acc_r[d].astype(bf16)
+                row_sum(d, False, True)
+
     def reduce_rows(t):
-        def one(d, up, ahead, first, landing, recv_sem):
-            @pl.when(both(ahead, first))
-            def _():
-                row_send[d] = acc_r[d].astype(bf16)
-
-            @pl.when(both(ahead, jnp.logical_not(first)))
+        def one(d, up, ahead, landing, recv_sem):
+            @pl.when(ahead)
             def _():
                 arrived(landing.at[d], recv_sem.at[d])
                 row_send[d] = (acc_r[d] + landing[d].astype(f32)).astype(bf16)
-
-            row_sum(d, up, True)
+                row_sum(d, up, True)
 
         up = n_col - 1 - t + c
         down = t - (n_col - 1) + c
-        one(up, True, both(c < up, up < n_col), c == 0, row_up, up_recv_sem)
-        one(down, False, both(c > down, down >= 0), c == n_col - 1, row_down, down_recv_sem)
-
-    to_cols(c)
-
-    @pl.loop(0, max(chips, n_col - 1))
+        one(up, True, both(0 < c, c < up, up < n_col), row_up, up_recv_sem)
+        one(
+            down, False, both(c < n_col - 1, c > down, down >= 0), row_down, down_recv_sem
+        )
+
+    gather_step(1)
+    rows_step(0, True)
+    to_cols(c, True)
+
+    @pl.loop(1, max(chips, n_col - 2))
     def _(j):
         rows_step(j)
 
@@ -332,13 +343,14 @@
         def _():
             gather_step(j + 1)
 
-    reduce_rows(0)
+    start_rows()
 
     @pl.loop(1, n_col - 1)
     def _(s):
         cols_step(s)
 
-    gather_step(n_col - 1)
+    if n_col > 2:
+        gather_step(n_col - 1)
     cols_step(n_col - 1)
 
     here = pl.ds(pl.multiple_of(q * rows, rows), rows)
@@ -348,6 +360,8 @@
     def _(kk):
         sib_send[kk] = acc_c[kk, :, there].astype(bf16)
         pair(kk, True)
+
+    reduce_rows(1)
 
     @pl.loop(0, k)
     def _(kk):
@@ -355,7 +369,7 @@
         col_send[kk] = (acc_c[kk, :, here] + sib_recv[kk].astype(f32)).astype(bf16)
         col_sum(kk).start()
 
-    @pl.loop(1, n_col - 1)
+    @pl.loop(2, n_col - 1)
     def _(t):
         reduce_rows(t)
 

time: 32.8 us -> 33.3 us (1.015)
  the two profiles are of different devices: /device:TPU:0 before, /device:TPU:6 now
where the time goes in v5:
time: 33.3 us; the launch traced here: 33.2 us
  Pallas kernels  30.9 us (93%)
  local copies, waits for them, and re-layouts  1.57 us (5%)
  between operations  0.66 us (2%)
    pallas_call x1, Pallas kernels, shards(): pl.pallas_call(functools.partial(kernel, n_row, n_col), out_shape=jax.Sha...  30.9 us
    unnamed x1, local copies, waits for them, and re-layouts  1.57 us

profile of v5, /device:TPU:6, one launch (start us, length us, event | category | flops | bytes accessed | tf_op | source)
XLA Modules:
  0.0 33.2 jit_solution(13995289892291459574)
XLA Ops:
  0.7 30.9 %gin_layer.1 = bf16[256,256]{1,0:T(8,128)(2,1)} custom-call(bf16[256,256]{1,0:T(8,128)(2,1)} %x_ref.1, bf16[1,96,128,128]{3,2,1,0:T(8,128)(2,1)} %adjacency_ref.1, s32[1,96]{1,0:T(1,128)} %tile_row_ref.1, s32[1,96]{1,0:T(1,128)} %tile_column_ref.1, s32[1]{0:T(128)S(6)} %copy.11.count_ref, bf16[256,1024]{1,0:T(8,128)(2,1)} %weight_in_ref.1, ...), custom_call_target="tpu_custom_call" | custom-call | tf_op jit(solution)/shard_map/gin_layer/pallas_call | solution.py:484
  31.6 1.6 %copy.12 = bf16[256,256]{1,0:T(8,128)(2,1)} copy(bf16[256,256]{1,0:T(8,128)(2,1)} %gin_layer.1) | data formatting | bytes 262144

commit v6 on v5

--- a/solution.py
+++ b/solution.py
@@ -301,20 +301,18 @@
             def _():
                 to_cols(source)
 
-    def start_rows():
+    def start_rows(t):
+        up = n_col - 1 - t
+
         @pl.when(c == 0)
         def _():
-            @pl.loop(1, n_col)
-            def _(s):
-                row_send[n_col - s] = acc_r[n_col - s].astype(bf16)
-                row_sum(n_col - s, True, True)
+            row_send[up] = acc_r[up].astype(bf16)
+            row_sum(up, True, True)
 
         @pl.when(c == n_col - 1)
         def _():
-            @pl.loop(0, n_col - 1)
-            def _(d):
-                row_send[d] = acc_r[d].astype(bf16)
-                row_sum(d, False, True)
+            row_send[t] = acc_r[t].astype(bf16)
+            row_sum(t, False, True)
 
     def reduce_rows(t):
         def one(d, up, ahead, landing, recv_sem):
@@ -343,11 +341,14 @@
         def _():
             gather_step(j + 1)
 
-    start_rows()
+    start_rows(0)
 
     @pl.loop(1, n_col - 1)
     def _(s):
         cols_step(s)
+
+    if n_col > 2:
+        start_rows(1)
 
     if n_col > 2:
         gather_step(n_col - 1)
@@ -360,6 +361,10 @@
     def _(kk):
         sib_send[kk] = acc_c[kk, :, there].astype(bf16)
         pair(kk, True)
+
+    @pl.loop(2, n_col - 1)
+    def _(t):
+        start_rows(t)
 
     reduce_rows(1)
 

time: 33.3 us -> 33.3 us (level)
  no operation moved by 1% of the time
where the time goes in v6:
time: 33.3 us; the launch traced here: 33.2 us
  Pallas kernels  30.9 us (93%)
  local copies, waits for them, and re-layouts  1.57 us (5%)
  between operations  0.66 us (2%)
    pallas_call x1, Pallas kernels, shards(): pl.pallas_call(functools.partial(kernel, n_row, n_col), out_shape=jax.Sha...  30.9 us
    unnamed x1, local copies, waits for them, and re-layouts  1.57 us

profile of v6, /device:TPU:6, one launch (start us, length us, event | category | flops | bytes accessed | tf_op | source)
XLA Modules:
  0.0 33.2 jit_solution(3789846699006138131)
XLA Ops:
  0.7 30.9 %gin_layer.1 = bf16[256,256]{1,0:T(8,128)(2,1)} custom-call(bf16[256,256]{1,0:T(8,128)(2,1)} %x_ref.1, bf16[1,96,128,128]{3,2,1,0:T(8,128)(2,1)} %adjacency_ref.1, s32[1,96]{1,0:T(1,128)} %tile_row_ref.1, s32[1,96]{1,0:T(1,128)} %tile_column_ref.1, s32[1]{0:T(128)S(6)} %copy.11.count_ref, bf16[256,1024]{1,0:T(8,128)(2,1)} %weight_in_ref.1, ...), custom_call_target="tpu_custom_call" | custom-call | tf_op jit(solution)/shard_map/gin_layer/pallas_call | solution.py:489
  31.6 1.6 %copy.12 = bf16[256,256]{1,0:T(8,128)(2,1)} copy(bf16[256,256]{1,0:T(8,128)(2,1)} %gin_layer.1) | data formatting | bytes 262144

commit v7 on v6

--- a/solution.py
+++ b/solution.py
@@ -9,6 +9,7 @@
 
 TILE = 128
 CORES = 2
+PIECES = 2
 MESH = pl.DeviceIdType.MESH
 
 
@@ -142,14 +143,21 @@
             start,
         )
 
+    def piece(p):
+        return pl.ds(p * (rows // PIECES), rows // PIECES)
+
     def row_sum(d, up, start):
+        for p in range(PIECES):
+            row_piece(d, p, up, start)
+
+    def row_piece(d, p, up, start):
         run(
             both(c < d, d < n_col) if up else both(c > d, d >= 0),
             lambda: remote(
-                row_send.at[d],
-                (row_up if up else row_down).at[d],
-                (up_send_sem if up else down_send_sem).at[d],
-                (up_recv_sem if up else down_recv_sem).at[d],
+                row_send.at[d, piece(p)],
+                (row_up if up else row_down).at[d, piece(p)],
+                (up_send_sem if up else down_send_sem).at[p, d],
+                (up_recv_sem if up else down_recv_sem).at[p, d],
                 above if up else below,
             ),
             start,
@@ -315,19 +323,23 @@
             row_sum(t, False, True)
 
     def reduce_rows(t):
-        def one(d, up, ahead, landing, recv_sem):
+        def one(d, p, up, ahead, landing, recv_sem):
             @pl.when(ahead)
             def _():
-                arrived(landing.at[d], recv_sem.at[d])
-                row_send[d] = (acc_r[d] + landing[d].astype(f32)).astype(bf16)
-                row_sum(d, up, True)
+                part = piece(p)
+                arrived(landing.at[d, part], recv_sem.at[p, d])
+                row_send[d, part] = (
+                    acc_r[d, part] + landing[d, part].astype(f32)
+                ).astype(bf16)
+                row_piece(d, p, up, True)
 
         up = n_col - 1 - t + c
         down = t - (n_col - 1) + c
-        one(up, True, both(0 < c, c < up, up < n_col), row_up, up_recv_sem)
-        one(
-            down, False, both(c < n_col - 1, c > down, down >= 0), row_down, down_recv_sem
-        )
+        ahead_up = both(0 < c, c < up, up < n_col)
+        ahead_down = both(c < n_col - 1, c > down, down >= 0)
+        for p in range(PIECES):
+            one(up, p, True, ahead_up, row_up, up_recv_sem)
+            one(down, p, False, ahead_down, row_down, down_recv_sem)
 
     gather_step(1)
     rows_step(0, True)
@@ -386,22 +398,26 @@
         arrived(sib_recv.at[k], pair_recv_sem.at[k])
         acc_c[k, :, here] += sib_recv[k].astype(f32)
 
-    @pl.when(c > 0)
-    def _():
-        arrived(row_up.at[c], up_recv_sem.at[c])
-        acc_r[c] += row_up[c].astype(f32)
-
-    @pl.when(c < n_col - 1)
-    def _():
-        arrived(row_down.at[c], down_recv_sem.at[c])
-        acc_r[c] += row_down[c].astype(f32)
-
     @pl.loop(k + 1, chips)
     def _(kk):
         arrived(col_recv.at[kk], col_recv_sem.at[kk])
         acc_c[k, :, here] += col_recv[kk].astype(f32)
 
-    combined = (x_ref[...].astype(f32) + acc_r[c] + acc_c[k, :, here].T).astype(bf16)
+    acc_r[c] += x_ref[...].astype(f32) + acc_c[k, :, here].T
+    for p in range(PIECES):
+        part = piece(p)
+
+        @pl.when(c > 0)
+        def _():
+            arrived(row_up.at[c, part], up_recv_sem.at[p, c])
+            acc_r[c, part] += row_up[c, part].astype(f32)
+
+        @pl.when(c < n_col - 1)
+        def _():
+            arrived(row_down.at[c, part], down_recv_sem.at[p, c])
+            acc_r[c, part] += row_down[c, part].astype(f32)
+
+    combined = acc_r[c].astype(bf16)
     hid = w_in.shape[1]
     part = min(hid, 256)
     total = jnp.zeros(out_ref.shape, f32) + bias_out_ref[...]
@@ -477,10 +493,10 @@
             dma((chips,)),
             dma((n_row,)),
             dma((chips,)),
-            dma((n_col,)),
-            dma((n_col,)),
-            dma((n_col,)),
-            dma((n_col,)),
+            dma((PIECES, n_col)),
+            dma((PIECES, n_col)),
+            dma((PIECES, n_col)),
+            dma((PIECES, n_col)),
             dma((chips,)),
             dma((chips,)),
             dma((chips,)),

time: 33.3 us -> 31.4 us (0.943)
  Pallas kernels: 30.9 us -> 29 us
    pallas_call x1, Pallas kernels: 30.9 us -> 29 us  [shards(): pl.pallas_call(functools.partial(kernel, n_row, n_col), out_shape=jax.Sha...]
where the time goes in v7:
time: 31.4 us; the launch traced here: 31.3 us
  Pallas kernels  29 us (92%)
  local copies, waits for them, and re-layouts  1.57 us (5%)
  between operations  0.66 us (2%)
    pallas_call x1, Pallas kernels, shards(): pl.pallas_call(functools.partial(kernel, n_row, n_col), out_shape=jax.Sha...  29 us
    unnamed x1, local copies, waits for them, and re-layouts  1.57 us

profile of v7, /device:TPU:6, one launch (start us, length us, event | category | flops | bytes accessed | tf_op | source)
XLA Modules:
  0.0 31.3 jit_solution(3541326745727701726)
XLA Ops:
  0.7 29.0 %gin_layer.1 = bf16[256,256]{1,0:T(8,128)(2,1)} custom-call(bf16[256,256]{1,0:T(8,128)(2,1)} %x_ref.1, bf16[1,96,128,128]{3,2,1,0:T(8,128)(2,1)} %adjacency_ref.1, s32[1,96]{1,0:T(1,128)} %tile_row_ref.1, s32[1,96]{1,0:T(1,128)} %tile_column_ref.1, s32[1]{0:T(128)S(6)} %copy.11.count_ref, bf16[256,1024]{1,0:T(8,128)(2,1)} %weight_in_ref.1, ...), custom_call_target="tpu_custom_call" | custom-call | tf_op jit(solution)/shard_map/gin_layer/pallas_call | solution.py:505
  29.7 1.6 %copy.12 = bf16[256,256]{1,0:T(8,128)(2,1)} copy(bf16[256,256]{1,0:T(8,128)(2,1)} %gin_layer.1) | data formatting | bytes 262144

commit v8 on v7

--- a/solution.py
+++ b/solution.py
@@ -9,7 +9,7 @@
 
 TILE = 128
 CORES = 2
-PIECES = 2
+PIECES = 4
 MESH = pl.DeviceIdType.MESH
 
 

time: 31.4 us -> 31.4 us (level)
  the two profiles are of different devices: /device:TPU:6 before, /device:TPU:0 now
where the time goes in v8:
time: 31.4 us; the launch traced here: 31.3 us
  Pallas kernels  29.1 us (93%)
  local copies, waits for them, and re-layouts  1.57 us (5%)
  between operations  0.66 us (2%)
    pallas_call x1, Pallas kernels, shards(): pl.pallas_call(functools.partial(kernel, n_row, n_col), out_shape=jax.Sha...  29.1 us
    unnamed x1, local copies, waits for them, and re-layouts  1.57 us

profile of v8, /device:TPU:0, one launch (start us, length us, event | category | flops | bytes accessed | tf_op | source)
XLA Modules:
  0.0 31.3 jit_solution(16707249638255657801)
XLA Ops:
  0.7 29.1 %gin_layer.1 = bf16[256,256]{1,0:T(8,128)(2,1)} custom-call(bf16[256,256]{1,0:T(8,128)(2,1)} %x_ref.1, bf16[1,96,128,128]{3,2,1,0:T(8,128)(2,1)} %adjacency_ref.1, s32[1,96]{1,0:T(1,128)} %tile_row_ref.1, s32[1,96]{1,0:T(1,128)} %tile_column_ref.1, s32[1]{0:T(128)S(6)} %copy.11.count_ref, bf16[256,1024]{1,0:T(8,128)(2,1)} %weight_in_ref.1, ...), custom_call_target="tpu_custom_call" | custom-call | tf_op jit(solution)/shard_map/gin_layer/pallas_call | solution.py:505
  29.7 1.6 %copy.12 = bf16[256,256]{1,0:T(8,128)(2,1)} copy(bf16[256,256]{1,0:T(8,128)(2,1)} %gin_layer.1) | data formatting | bytes 262144
